TPU v7x, 32 devices: a whole 2x2x4 slice. The times are simulated.
32 devices in a mesh: dp: 8 (over y, x, core), mp: 4 (over z).
Axes of the slice: x: 2, y: 2, z: 4, core: 2. Of those that a mesh axis runs over, the one named last changes fastest.
Arguments:
- inputs: bfloat16 [16384, 1024], P('mp', 'dp'), may hold values from -6 to 6
- cotangent: bfloat16 [16384, 1024], P('mp', 'dp'), may hold values from -6 to 6
- r_factor: bfloat16 [1, 128, 128, 128], P(None, 'mp'), may hold values from -0.5 to 0.5
- l_factor: bfloat16 [1, 128, 128, 128], P(None, 'mp'), may hold values from -0.5 to 0.5
Outputs:
- outputs: bfloat16 [16384, 1024], P('mp', 'dp')
- grad_inputs: bfloat16 [16384, 1024], P('mp', 'dp')
- grad_r: float32 [1, 128, 128, 128], P(None, 'mp', 'dp')
- grad_l: float32 [1, 128, 128, 128], P(None, 'mp', 'dp')
All inputs are finite; a program needn't handle non-finite values.
Results may differ from a plain program's by a relative error of at most 0.0063.
Values may be sent and summed in bfloat16 or wider, within the bound.
A program may use at most 64 MiB of HBM per device.

v0:
```python
import jax
import jax.numpy as jnp
from jax import lax
from jax.sharding import PartitionSpec as P

LAYERS = 1


def activate(values):
    return jax.nn.gelu(values, approximate=True)


def second_product(received, left):
    return jnp.einsum("ijt,jim->jmt", received, left, preferred_element_type=jnp.float32)


def left_apply(left, received):
    return (received, second_product(received, left))


def first_product(current, right):
    return jnp.einsum("ikt,ikj->ijt", current, right, preferred_element_type=jnp.float32).astype(
        jnp.bfloat16
    )


def forward_layer(current, right, left):
    first_out = first_product(current, right)
    return left_apply(
        left, lax.all_to_all(first_out, "mp", split_axis=1, concat_axis=0, tiled=True)
    )


def shards(inputs, cotangent, r_factor, l_factor):
    block_count = r_factor.shape[1]
    block_size = r_factor.shape[2]
    tokens_here = inputs.shape[1]
    scale = float(lax.axis_size("dp") * tokens_here) ** (-0.5)
    current = inputs.reshape(block_count, block_size, tokens_here)
    layer_index = 0
    received, pre_act = forward_layer(current, r_factor[layer_index], l_factor[layer_index])
    saved = [(current, received, pre_act)]
    current = activate(pre_act).astype(jnp.bfloat16)
    outputs = current.reshape(block_count * block_size, tokens_here)
    grad_now = cotangent.reshape(block_count, block_size, tokens_here)
    parts_r = [None] * LAYERS
    parts_l = [None] * LAYERS
    for layer_index in reversed(range(LAYERS)):
        right = r_factor[layer_index]
        left = l_factor[layer_index]
        layer_in = saved[layer_index][0]
        received = saved[layer_index][1]
        pre_act = saved[layer_index][2]
        back_fn = jax.vjp(activate, pre_act)[1]
        grad_pre = back_fn(grad_now.astype(jnp.float32))[0].astype(jnp.bfloat16)
        term_l = (
            jnp.einsum("ijt,jmt->jim", received, grad_pre, preferred_element_type=jnp.float32)
            * scale
        )
        parts_l[layer_index] = lax.psum_scatter(term_l, "dp", scatter_dimension=1, tiled=True)
        grad_first = jnp.einsum(
            "jmt,jim->ijt", grad_pre, left, preferred_element_type=jnp.float32
        ).astype(jnp.bfloat16)

        def apply_back(returned, right=right):
            spread = jnp.einsum("ijt,ikj->ikt", returned, right, preferred_element_type=jnp.float32)
            return (returned, spread.astype(jnp.bfloat16))

        returned, grad_now = apply_back(
            lax.all_to_all(grad_first, "mp", split_axis=0, concat_axis=1, tiled=True)
        )
        term_r = (
            jnp.einsum("ikt,ijt->ikj", layer_in, returned, preferred_element_type=jnp.float32)
            * scale
        )
        parts_r[layer_index] = lax.psum_scatter(term_r, "dp", scatter_dimension=1, tiled=True)
    stack_r = jnp.stack(parts_r, 0)
    stack_l = jnp.stack(parts_l, 0)
    grad_inputs = grad_now.reshape(block_count * block_size, tokens_here)
    return (outputs, grad_inputs, stack_r, stack_l)


def solution(mesh):
    placed = (P("mp", "dp"), P("mp", "dp"), P(None, "mp", None, None), P(None, "mp", None, None))
    return jax.shard_map(
        shards,
        mesh=mesh,
        in_specs=placed,
        out_specs=(
            P("mp", "dp"),
            P("mp", "dp"),
            P(None, "mp", "dp", None),
            P(None, "mp", "dp", None),
        ),
        check_vma=False,
    )
```

profile of v0, /device:TPU:0, one launch (start us, length us, event | category | flops | bytes accessed | tf_op | source)
XLA Modules:
  0.0 174.5 jit_solution(9278482145259703794)
XLA Ops:
  7.2 0.0 copy-start
  7.2 0.0 reduce-scatter.3.cloned.1.call-start
  7.2 2.1 %convolution_convert_fusion.2 = bf16[32,128,128]{2,1,0:T(8,128)(2,1)S(1)} fusion(bf16[32,128,128]{2,1,0:T(8,128)(2,1)} %bitcast.56, bf16[1,32,128,128]{3,2,1,0:T(8,128)(2,1)} %param.6), kind=kOutput, calls=%fused_computation.20 | convolution fusion | flops 134742016 | bytes 3145728 | tf_op jit(solution)/shard_map/ikt,ikj->ijt/dot_general | solution.py:22
  9.4 0.7 copy.22
  10.1 0.0 copy-start.4
  10.1 32.0 %all_to_all.36 = bf16[32,128,128]{2,0,1:T(8,128)(2,1)S(1)} all-to-all(bf16[32,128,128]{2,0,1:T(8,128)(2,1)S(1)} %copy.22), channel_id=1, replica_groups=mesh['dp'=8,'mp'=4] {'mp'}, dimensions={1} | all-to-all | bytes 2097152 | tf_op jit(solution)/shard_map/all_to_all | solution.py:30
  42.0 0.1 copy.23
  42.2 0.0 copy-start.3
  42.2 0.0 copy-done
  42.2 0.0 copy-done.4
  42.2 3.0 %fusion.2 = (bf16[32,128,128]{2,1,0:T(8,128)(2,1)S(1)}, bf16[32,128,128]{2,1,0:T(8,128)(2,1)}) fusion(bf16[32,128,128]{2,1,0:T(8,128)(2,1)S(1)} %bitcast.64, bf16[128,32,128]{2,0,1:T(8,128)(2,1)S(1)} %bitcast.60, bf16[1,32,128,128]{3,2,1,0:T(8,128)(2,1)S(1)} %copy-done), kind=kOutput, calls=%fused_computation.6 | convolution fusion | flops 146276352 | bytes 5242880 | tf_op jit(solution)/shard_map/ijt,jim->jmt/dot_general | solution.py:14
  45.2 0.0 copy-done.3
  45.2 0.9 fusion.11
  46.1 1.7 copy.26
  47.8 0.0 copy-start.2
  47.8 28.5 %all_to_all.37 = bf16[128,32,128]{2,1,0:T(8,128)(2,1)S(1)} all-to-all(bf16[128,32,128]{2,1,0:T(8,128)(2,1)} %copy.26), channel_id=1, replica_groups=mesh['dp'=8,'mp'=4] {'mp'}, dimensions={0} | all-to-all | bytes 2097152 | tf_op jit(solution)/shard_map/all_to_all | solution.py:70
  76.2 0.1 copy.27
  76.4 0.0 copy-done.2
  76.4 2.2 %multiply_bitcast_fusion = f32[32,128,128]{1,2,0:T(8,128)} fusion(bf16[32,128,128]{2,1,0:T(8,128)(2,1)S(1)} %bitcast.54, bf16[32,128,128]{2,1,0:T(8,128)(2,1)S(1)} %bitcast.57), kind=kOutput, calls=%fused_computation.16 | convolution fusion | flops 134742016 | bytes 4194304 | tf_op jit(solution)/shard_map/ikt,ijt->ikj/dot_general | solution.py:73
  78.6 3.1 %copy.28 = f32[32,128,128]{2,0,1:T(8,128)} copy(f32[32,128,128]{1,2,0:T(8,128)} %multiply_bitcast_fusion) | data formatting | bytes 4194304 | tf_op jit(solution)/shard_map/mul | solution.py:73
  81.7 0.0 reduce-scatter.3.cloned.1.call-update
  81.7 0.0 reduce-scatter.5.cloned.1.call-start
  81.8 3.4 %convolution_multiply_fusion = f32[32,128,128]{2,1,0:T(8,128)} fusion(bf16[128,32,128]{2,0,1:T(8,128)(2,1)} %bitcast.61, bf16[32,128,128]{2,1,0:T(8,128)(2,1)S(1)} %get-tuple-element.16), kind=kOutput, calls=%fused_computation.17 | convolution fusion | flops 134742016 | bytes 4194304 | tf_op jit(solution)/shard_map/ijt,jmt->jim/dot_general | solution.py:57
  85.2 0.0 copy-start.1
  85.2 0.0 reduce-scatter.5.cloned.1.call-update
  85.2 1.2 copy-done.1
  86.4 1.4 convolution_convert_fusion
  87.8 34.4 %reduce-scatter.3.cloned.1.call-done = f32[32,16,128]{2,0,1:T(8,128)} async-done(((f32[32,128,128]{2,0,1:T(8,128)}), f32[32,16,128]{2,0,1:T(8,128)}) %reduce-scatter.3.cloned.1.call-update) | async-done | bytes 262160 | tf_op jit(solution)/shard_map/reduce_scatter | solution.py:76
  122.2 1.8 %copy.29 = f32[1,32,16,128]{3,2,1,0:T(8,128)} copy(f32[1,32,16,128]{3,1,2,0:T(8,128)} %bitcast.63) | data formatting | bytes 524288
  124.0 43.7 %reduce-scatter.5.cloned.1.call-done = f32[32,16,128]{2,1,0:T(8,128)} async-done(((f32[32,128,128]{2,1,0:T(8,128)}), f32[32,16,128]{2,1,0:T(8,128)}) %reduce-scatter.5.cloned.1.call-update) | async-done | bytes 262160 | tf_op jit(solution)/shard_map/reduce_scatter | solution.py:60
Async XLA Ops:
  7.2 35.0 %copy-start = (bf16[1,32,128,128]{3,2,1,0:T(8,128)(2,1)S(1)}, bf16[1,32,128,128]{3,2,1,0:T(8,128)(2,1)}, u32[]{:S(2)}) copy-start(bf16[1,32,128,128]{3,2,1,0:T(8,128)(2,1)} %param.7) | copy-start | bytes 3145732
  7.2 115.0 %reduce-scatter.3.cloned.1.call-start = ((), (), s32[]{:S(2)}) async-start(), calls=%async_computation.4 | async-start | bytes 2359296 | tf_op jit(solution)/shard_map/reduce_scatter | solution.py:76
  10.1 32.1 %copy-start.4 = (bf16[4096,128]{1,0:T(8,128)(2,1)S(1)}, bf16[4096,128]{1,0:T(8,128)(2,1)}, u32[]{:S(2)}) copy-start(bf16[4096,128]{1,0:T(8,128)(2,1)} %param.5) | copy-start | bytes 3145732
  42.2 3.0 %copy-start.3 = (bf16[32,4,32,128]{3,0,1,2:T(8,128)(2,1)}, bf16[32,4,32,128]{3,0,1,2:T(8,128)(2,1)S(1)}, u32[]{:S(2)}) copy-start(bf16[32,4,32,128]{3,0,1,2:T(8,128)(2,1)S(1)} %copy.23) | copy-start | bytes 3145732
  47.8 28.6 %copy-start.2 = (bf16[4096,128]{1,0:T(8,128)(2,1)S(1)}, bf16[4096,128]{1,0:T(8,128)(2,1)}, u32[]{:S(2)}) copy-start(bf16[4096,128]{1,0:T(8,128)(2,1)} %param.4) | copy-start | bytes 3145732
  81.7 86.0 %reduce-scatter.5.cloned.1.call-start = ((), (), s32[]{:S(2)}) async-start(), calls=%async_computation.5 | async-start | bytes 2359296 | tf_op jit(solution)/shard_map/reduce_scatter | solution.py:60
  85.2 1.2 copy-start.1
Sparse Core Ops, SparseCore 0:
  81.8 40.3 reduce-scatter.2
  126.4 41.2 reduce-scatter.4
where the time goes:
time: 175 us
  waiting for transfers between devices  78.1 us (45%)
  blocking collectives  60.5 us (35%)
  between operations  14.1 us (8%)
  matrix products  13 us (7%)
  local copies, waits for them, and re-layouts  8.8 us (5%)
    reduce_scatter x1, waiting for transfers between devices, shards(): lax.psum_scatter(term_l, 'dp', scatter_dimension=1, tiled=True)  43.7 us
    reduce_scatter x1, waiting for transfers between devices, shards(): lax.psum_scatter(term_r, 'dp', scatter_dimension=1, tiled=True)  34.4 us
    all_to_all x1, blocking collectives, forward_layer(): lax.all_to_all(first_out, 'mp', split_axis=1, concat_axis=0, tiled=True)  32 us
    all_to_all x1, blocking collectives, shards(): lax.all_to_all(grad_first, 'mp', split_axis=0, concat_axis=1, tiled=True)  28.5 us
  transfers between devices with their start and end apart: 2, of which 2 were waited for; matrix products, arithmetic and copies ran while one was open for 4% of the time, Pallas kernels for 0%

commit v1 on v0

v1 whole, which is shorter than its diff:
```python
import functools

import jax
import jax.numpy as jnp
from jax import lax
from jax.experimental import pallas as pl
from jax.experimental.pallas import tpu as pltpu
from jax.sharding import PartitionSpec as P

MESH = pl.DeviceIdType.MESH
F32 = jnp.float32
BF16 = jnp.bfloat16


def dot(left, right, left_dim, right_dim):
    return lax.dot_general(
        left, right, (((left_dim,), (right_dim,)), ((), ())), preferred_element_type=F32
    )


def gelu_and_slope(v):
    c0, c1 = 0.7978845608028654, 0.044715
    square = v * v
    tanh = jnp.tanh(c0 * v * (1.0 + c1 * square))
    half = 0.5 + 0.5 * tanh
    slope = half + 0.5 * v * (1.0 - tanh * tanh) * (c0 + (3.0 * c0 * c1) * square)
    return v * half, slope


def remote(src, dst, send_sem, recv_sem, axis, target):
    return pltpu.make_async_remote_copy(
        src_ref=src,
        dst_ref=dst,
        send_sem=send_sem,
        recv_sem=recv_sem,
        device_id={axis: target},
        device_id_type=MESH,
    )


def kernel(
    cfg,
    a_hbm, g_hbm, r_hbm, l_hbm,
    out_hbm, gi_hbm, gr_hbm, gl_hbm,
    a_v, g_v, r_v, l_v,
    fo32, fs, fr,
    gf32, gs, gb,
    out_v, gi_v,
    tl_s, tl_r, tr_s, tr_r,
    gl_v, gr_v,
    in_sem, out_sem,
    fs_sem, fr_sem, gs_sem, gb_sem,
    ls_sem, lr_sem, rs_sem, rr_sem,
):
    M, D, nb, B, T, rows, scale, NC, H, G = cfg
    jc, hj, ic = nb // NC, nb // H, nb // G
    mp, dp = lax.axis_index("mp"), lax.axis_index("dp")

    loads = [
        pltpu.make_async_copy(src, dst, in_sem.at[n])
        for n, (src, dst) in enumerate(
            ((a_hbm, a_v), (r_hbm, r_v), (l_hbm, l_v), (g_hbm, g_v))
        )
    ]
    for load in loads:
        load.start()

    barrier = pltpu.get_barrier_semaphore()
    for s in range(1, M):
        pl.semaphore_signal(
            barrier, inc=1, device_id={"mp": lax.rem(mp + s, M)}, device_id_type=MESH
        )
    for s in range(1, D):
        pl.semaphore_signal(
            barrier, inc=1, device_id={"dp": lax.rem(dp + s, D)}, device_id_type=MESH
        )

    loads[0].wait()
    loads[1].wait()

    def first(i, carry):
        fo32[pl.ds(i, B, stride=nb), :] = dot(r_v[i], a_v[i], 0, 0)
        return carry

    lax.fori_loop(0, nb, first, 0, unroll=4)
    pl.semaphore_wait(barrier, (M - 1) + (D - 1))

    mine = pl.multiple_of(mp * nb, nb)
    forward = []
    for c in range(NC):
        step = []
        for s in range(1, M):
            target = lax.rem(mp + s, M)
            base = target * nb + c * jc

            def pack(j, carry, base=base):
                at = pl.multiple_of((base + j) * nb, nb)
                fs[base + j] = fo32[pl.ds(at, nb), :].astype(BF16)
                return carry

            lax.fori_loop(0, jc, pack, 0, unroll=4)
            copy = remote(
                fs.at[pl.ds(base, jc)],
                fr.at[pl.ds(c * jc, jc), pl.ds(mine, nb)],
                fs_sem.at[c, s - 1],
                fr_sem.at[c, s - 1],
                "mp",
                target,
            )
            copy.start()
            step.append(copy)
        forward.append(step)

    def own(j, carry):
        at = pl.multiple_of((mine + j) * nb, nb)
        fr[j, pl.ds(mine, nb), :] = fo32[pl.ds(at, nb), :].astype(BF16)
        return carry

    lax.fori_loop(0, nb, own, 0, unroll=4)
    loads[2].wait()
    loads[3].wait()

    def second(jj, carry):
        x, left = fr[jj], l_v[jj]
        value, slope = gelu_and_slope(dot(left, x, 0, 0))
        out_v[jj] = value.astype(BF16)
        grad_pre = (g_v[jj].astype(F32) * slope).astype(BF16)
        gf32[pl.ds(pl.multiple_of(jj * B, B), B), :] = dot(left, grad_pre, 1, 0)
        term = (dot(x, grad_pre, 1, 1) * scale).astype(BF16)
        for d in range(D):
            tl_s[d, jj] = term[d * rows : (d + 1) * rows]
        return carry

    back, sums_l = [], []
    per_half = NC // H
    for h in range(H):
        for c in range(h * per_half, (h + 1) * per_half):
            for copy in forward[c]:
                copy.wait_recv()
            lax.fori_loop(c * jc, (c + 1) * jc, second, 0, unroll=2)

        at_j = pl.multiple_of(mine + h * hj, hj)
        for g in range(G):
            for s in range(1, M):
                target = lax.rem(mp + s, M)
                base = target * nb + g * ic

                def turn(i, carry, base=base):
                    part = gf32[pl.ds(h * hj * B + base + i, hj, stride=B), :]
                    gs[base + i, pl.ds(h * hj, hj), :] = part.astype(BF16)
                    return carry

                lax.fori_loop(0, ic, turn, 0, unroll=4)
                copy = remote(
                    gs.at[pl.ds(base, ic), pl.ds(h * hj, hj)],
                    gb.at[pl.ds(g * ic, ic), pl.ds(at_j, hj)],
                    gs_sem.at[h * G + g, s - 1],
                    gb_sem.at[h * G + g, s - 1],
                    "mp",
                    target,
                )
                copy.start()
                back.append((g, copy))

        def turn_own(i, carry):
            part = gf32[pl.ds(h * hj * B + mine + i, hj, stride=B), :]
            gb[i, pl.ds(at_j, hj), :] = part.astype(BF16)
            return carry

        lax.fori_loop(0, nb, turn_own, 0, unroll=4)
        for s in range(1, D):
            target = lax.rem(dp + s, D)
            copy = remote(
                tl_s.at[target, pl.ds(h * hj, hj)],
                tl_r.at[s - 1, pl.ds(h * hj, hj)],
                ls_sem.at[h, s - 1],
                lr_sem.at[h, s - 1],
                "dp",
                target,
            )
            copy.start()
            sums_l.append(copy)

    stores = [pltpu.make_async_copy(out_v, out_hbm, out_sem.at[0])]
    stores[0].start()

    def add_l(jj, carry):
        total = tl_s[dp, jj].astype(F32)
        for s in range(D - 1):
            total = total + tl_r[s, jj].astype(F32)
        gl_v[jj] = total
        return carry

    for copy in sums_l:
        copy.wait_recv()
    lax.fori_loop(0, nb, add_l, 0, unroll=2)
    stores.append(pltpu.make_async_copy(gl_v, gl_hbm, out_sem.at[1]))
    stores[-1].start()

    def last(ii, carry):
        y = gb[ii]
        gi_v[ii] = dot(r_v[ii], y, 1, 0).astype(BF16)
        term = (dot(a_v[ii], y, 1, 1) * scale).astype(BF16)
        for d in range(D):
            tr_s[d, ii] = term[d * rows : (d + 1) * rows]
        return carry

    sums_r = []
    for g in range(G):
        for group, copy in back:
            if group == g:
                copy.wait_recv()
        lax.fori_loop(g * ic, (g + 1) * ic, last, 0, unroll=2)
        step = []
        for s in range(1, D):
            target = lax.rem(dp + s, D)
            copy = remote(
                tr_s.at[target, pl.ds(g * ic, ic)],
                tr_r.at[s - 1, pl.ds(g * ic, ic)],
                rs_sem.at[g, s - 1],
                rr_sem.at[g, s - 1],
                "dp",
                target,
            )
            copy.start()
            step.append(copy)
        sums_r.append(step)
    stores.append(pltpu.make_async_copy(gi_v, gi_hbm, out_sem.at[2]))
    stores[-1].start()

    def add_r(ii, carry):
        total = tr_s[dp, ii].astype(F32)
        for s in range(D - 1):
            total = total + tr_r[s, ii].astype(F32)
        gr_v[ii] = total
        return carry

    for g in range(G):
        for copy in sums_r[g]:
            copy.wait_recv()
        lax.fori_loop(g * ic, (g + 1) * ic, add_r, 0, unroll=2)
    stores.append(pltpu.make_async_copy(gr_v, gr_hbm, out_sem.at[3]))
    stores[-1].start()

    for step in forward + sums_r:
        for copy in step:
            copy.wait_send()
    for _, copy in back:
        copy.wait_send()
    for copy in sums_l:
        copy.wait_send()
    for store in stores:
        store.wait()


def fused(M, D, inputs, cotangent, r_factor, l_factor):
    nb, B = r_factor.shape[1], r_factor.shape[2]
    T = inputs.shape[1]
    rows = B // D
    scale = float(D * T) ** (-0.5)
    NC, H, G = 4, 2, 4
    cfg = (M, D, nb, B, T, rows, scale, NC, H, G)
    sem = pltpu.SemaphoreType.DMA
    flops = 6 * 2 * nb * B * B * T
    outputs, grad_inputs, grad_r, grad_l = pl.pallas_call(
        functools.partial(kernel, cfg),
        out_shape=(
            jax.ShapeDtypeStruct((nb, B, T), BF16),
            jax.ShapeDtypeStruct((nb, B, T), BF16),
            jax.ShapeDtypeStruct((nb, rows, B), F32),
            jax.ShapeDtypeStruct((nb, rows, B), F32),
        ),
        in_specs=[pl.BlockSpec(memory_space=pl.ANY)] * 4,
        out_specs=[pl.BlockSpec(memory_space=pl.ANY)] * 4,
        scratch_shapes=[
            pltpu.VMEM((nb, B, T), BF16),
            pltpu.VMEM((nb, B, T), BF16),
            pltpu.VMEM((nb, B, B), BF16),
            pltpu.VMEM((nb, B, B), BF16),
            pltpu.VMEM((B * nb, T), F32),
            pltpu.VMEM((B, nb, T), BF16),
            pltpu.VMEM((nb, B, T), BF16),
            pltpu.VMEM((nb * B, T), F32),
            pltpu.VMEM((B, nb, T), BF16),
            pltpu.VMEM((nb, B, T), BF16),
            pltpu.VMEM((nb, B, T), BF16),
            pltpu.VMEM((nb, B, T), BF16),
            pltpu.VMEM((D, nb, rows, B), BF16),
            pltpu.VMEM((D - 1, nb, rows, B), BF16),
            pltpu.VMEM((D, nb, rows, B), BF16),
            pltpu.VMEM((D - 1, nb, rows, B), BF16),
            pltpu.VMEM((nb, rows, B), F32),
            pltpu.VMEM((nb, rows, B), F32),
            sem((4,)),
            sem((4,)),
            sem((NC, M - 1)),
            sem((NC, M - 1)),
            sem((H * G, M - 1)),
            sem((H * G, M - 1)),
            sem((H, D - 1)),
            sem((H, D - 1)),
            sem((G, D - 1)),
            sem((G, D - 1)),
        ],
        compiler_params=pltpu.CompilerParams(
            collective_id=0, has_side_effects=True, vmem_limit_bytes=48 * 2**20
        ),
        cost_estimate=pl.CostEstimate(
            flops=flops, bytes_accessed=8 * nb * B * T * 2, transcendentals=nb * B * T
        ),
        name="monarch",
    )(
        inputs.reshape(nb, B, T),
        cotangent.reshape(nb, B, T),
        r_factor[0],
        l_factor[0],
    )
    return (
        outputs.reshape(nb * B, T),
        grad_inputs.reshape(nb * B, T),
        grad_r[None],
        grad_l[None],
    )


def plain(M, D, inputs, cotangent, r_factor, l_factor):
    nb, B = r_factor.shape[1], r_factor.shape[2]
    T = inputs.shape[1]
    scale = float(D * T) ** (-0.5)
    right, left = r_factor[0], l_factor[0]
    current = inputs.reshape(nb, B, T)
    first_out = jnp.einsum("ikt,ikj->ijt", current, right, preferred_element_type=F32)
    received = lax.all_to_all(
        first_out.astype(BF16), "mp", split_axis=1, concat_axis=0, tiled=True
    )
    pre_act = jnp.einsum("ijt,jim->jmt", received, left, preferred_element_type=F32)
    value, slope = gelu_and_slope(pre_act)
    grad_pre = (cotangent.reshape(nb, B, T).astype(F32) * slope).astype(BF16)
    term_l = jnp.einsum("ijt,jmt->jim", received, grad_pre, preferred_element_type=F32)
    grad_l = lax.psum_scatter(term_l * scale, "dp", scatter_dimension=1, tiled=True)
    grad_first = jnp.einsum("jmt,jim->ijt", grad_pre, left, preferred_element_type=F32)
    returned = lax.all_to_all(
        grad_first.astype(BF16), "mp", split_axis=0, concat_axis=1, tiled=True
    )
    spread = jnp.einsum("ijt,ikj->ikt", returned, right, preferred_element_type=F32)
    term_r = jnp.einsum("ikt,ijt->ikj", current, returned, preferred_element_type=F32)
    grad_r = lax.psum_scatter(term_r * scale, "dp", scatter_dimension=1, tiled=True)
    return (
        value.astype(BF16).reshape(nb * B, T),
        spread.astype(BF16).reshape(nb * B, T),
        grad_r[None],
        grad_l[None],
    )


def solution(mesh):
    M, D = mesh.shape["mp"], mesh.shape["dp"]

    def shards(inputs, cotangent, r_factor, l_factor):
        nb, B = r_factor.shape[1], r_factor.shape[2]
        tiled = nb % 32 == 0 and (B // D) % 16 == 0 and M > 1 and D > 1
        return (fused if tiled else plain)(M, D, inputs, cotangent, r_factor, l_factor)

    return jax.shard_map(
        shards,
        mesh=mesh,
        in_specs=(P("mp", "dp"), P("mp", "dp"), P(None, "mp"), P(None, "mp")),
        out_specs=(P("mp", "dp"), P("mp", "dp"), P(None, "mp", "dp"), P(None, "mp", "dp")),
        check_vma=False,
    )
```

time: 175 us -> 71 us (0.41)
  waiting for transfers between devices: 78.1 us -> 0 us
  Pallas kernels: 0 us -> 63.1 us
  blocking collectives: 60.5 us -> 0 us
  between operations: 14.1 us -> 0.65 us
  matrix products: 13 us -> 0 us
  local copies, waits for them, and re-layouts: 8.8 us -> 7.01 us
    reduce_scatter x2 -> x0, waiting for transfers between devices: 78.1 us -> none  [the longest x1 43.7 us: shards(): lax.psum_scatter(term_l, 'dp', scatter_dimension=1, tiled=True)]
    pallas_call x0 -> x1, Pallas kernels: none -> 63.1 us  [fused(): pl.pallas_call(functools.partial(kernel, cfg), out_shape=(jax.ShapeDtypeS...]
    all_to_all x2 -> x0, blocking collectives: 60.5 us -> none  [the longest x1 32 us: forward_layer(): lax.all_to_all(first_out, 'mp', split_axis=1, concat_axis=0, tiled=True)]
    dot_general x6 -> x0, matrix products: 13 us -> none  [the longest x1 3.38 us: shards(): jnp.einsum('ijt,jmt->jim', received, grad_pre, preferred_element_type=jnp...]
    unnamed x11 -> x10, local copies, waits for them, and re-layouts: 3.05 us -> 7.01 us
    mul x1 -> x0, local copies, waits for them, and re-layouts: 3.14 us -> none  [shards(): jnp.einsum('ikt,ijt->ikj', layer_in, returned, preferred_element_type=jnp...]
    convert_element_type x2 -> x0, local copies, waits for them, and re-layouts: 2.36 us -> none  [the longest x1 1.68 us: shards(): grad_first = jnp.einsum('jmt,jim->ijt', grad_pre, left, preferred_element...]
  transfers between devices with their start and end apart: 2 -> 0, of which waited for: 2 -> 0; matrix products, arithmetic and copies ran while one was open for 4% -> 0% of each run, Pallas kernels for 0% -> 0%
where the time goes in v1:
time: 71 us; the launch traced here: 70.8 us
  Pallas kernels  63.1 us (89%)
  local copies, waits for them, and re-layouts  7.01 us (10%)
    pallas_call x1, Pallas kernels, fused(): pl.pallas_call(functools.partial(kernel, cfg), out_shape=(jax.ShapeDtypeS...  63.1 us
    unnamed x10, local copies, waits for them, and re-layouts  7.01 us

profile of v1, /device:TPU:0, one launch (start us, length us, event | category | flops | bytes accessed | tf_op | source)
XLA Modules:
  0.0 70.8 jit_solution(14187039065752575414)
XLA Ops:
  0.6 0.0 copy-start
  0.6 1.2 %copy-done = bf16[4096,128]{1,0:T(8,128)(2,1)S(1)} copy-done((bf16[4096,128]{1,0:T(8,128)(2,1)S(1)}, bf16[4096,128]{1,0:T(8,128)(2,1)}, u32[]{:S(2)}) %copy-start) | copy-done | bytes 1048600
  1.9 0.0 copy-start.1
  1.9 1.2 %copy-done.1 = bf16[4096,128]{1,0:T(8,128)(2,1)S(1)} copy-done((bf16[4096,128]{1,0:T(8,128)(2,1)S(1)}, bf16[4096,128]{1,0:T(8,128)(2,1)}, u32[]{:S(2)}) %copy-start.1) | copy-done | bytes 1048600
  3.1 0.0 copy-start.2
  3.1 1.2 %copy-done.2 = bf16[1,32,128,128]{3,2,1,0:T(8,128)(2,1)S(1)} copy-done((bf16[1,32,128,128]{3,2,1,0:T(8,128)(2,1)S(1)}, bf16[1,32,128,128]{3,2,1,0:T(8,128)(2,1)}, u32[]{:S(2)}) %copy-start.2) | copy-done | bytes 1048600
  4.3 63.1 %monarch.1 = (bf16[32,128,128]{2,1,0:T(8,128)(2,1)S(1)}, bf16[32,128,128]{2,1,0:T(8,128)(2,1)S(1)}, f32[32,16,128]{2,1,0:T(8,128)S(1)}, f32[32,16,128]{2,1,0:T(8,128)S(1)}) custom-call(bf16[32,128,128]{2,1,0:T(8,128)(2,1)S(1)} %bitcast.10, bf16[32,128,128]{2,1,0:T(8,128)(2,1)S(1)} %bitcast.11, bf16[32,128,128]{2,1,0:T(8,128)(2,1)S(1)} %bitcast.12, ...), custom_call_target="tpu_custom_call" | custom-call | flops 805306368 | bytes 8388608 | tf_op jit(solution)/shard_map/monarch/pallas_call | solution.py:265
  67.4 1.0 %copy.12 = bf16[4096,128]{1,0:T(8,128)(2,1)} copy(bf16[4096,128]{1,0:T(8,128)(2,1)S(1)} %bitcast.9) | data formatting | bytes 2097152
  68.4 1.0 %copy.13 = bf16[4096,128]{1,0:T(8,128)(2,1)} copy(bf16[4096,128]{1,0:T(8,128)(2,1)S(1)} %bitcast.8) | data formatting | bytes 2097152
  69.4 0.7 copy.14
  70.1 0.7 copy.15
Async XLA Ops:
  0.6 1.2 %copy-start = (bf16[4096,128]{1,0:T(8,128)(2,1)S(1)}, bf16[4096,128]{1,0:T(8,128)(2,1)}, u32[]{:S(2)}) copy-start(bf16[4096,128]{1,0:T(8,128)(2,1)} %param.4) | copy-start | bytes 3145732
  1.9 1.2 %copy-start.1 = (bf16[4096,128]{1,0:T(8,128)(2,1)S(1)}, bf16[4096,128]{1,0:T(8,128)(2,1)}, u32[]{:S(2)}) copy-start(bf16[4096,128]{1,0:T(8,128)(2,1)} %param.5) | copy-start | bytes 3145732
  3.1 1.2 %copy-start.2 = (bf16[1,32,128,128]{3,2,1,0:T(8,128)(2,1)S(1)}, bf16[1,32,128,128]{3,2,1,0:T(8,128)(2,1)}, u32[]{:S(2)}) copy-start(bf16[1,32,128,128]{3,2,1,0:T(8,128)(2,1)} %param.6) | copy-start | bytes 3145732

commit v2 on v1

--- a/solution.py
+++ b/solution.py
@@ -10,6 +10,7 @@
 MESH = pl.DeviceIdType.MESH
 F32 = jnp.float32
 BF16 = jnp.bfloat16
+AHEAD = 2
 
 
 def dot(left, right, left_dim, right_dim):
@@ -56,14 +57,18 @@
     jc, hj, ic = nb // NC, nb // H, nb // G
     mp, dp = lax.axis_index("mp"), lax.axis_index("dp")
 
-    loads = [
-        pltpu.make_async_copy(src, dst, in_sem.at[n])
-        for n, (src, dst) in enumerate(
-            ((a_hbm, a_v), (r_hbm, r_v), (l_hbm, l_v), (g_hbm, g_v))
-        )
-    ]
-    for load in loads:
-        load.start()
+    half = nb // 2
+    loads = []
+    for src, dst, parts in (
+        (a_hbm, a_v, 2), (r_hbm, r_v, 2), (l_hbm, l_v, 1), (g_hbm, g_v, 1)
+    ):
+        for p in range(parts):
+            at = pl.ds(p * (nb // parts), nb // parts)
+            loads.append(
+                pltpu.make_async_copy(src.at[at], dst.at[at], in_sem.at[len(loads)])
+            )
+    for n in (0, 2, 1, 3, 4, 5):
+        loads[n].start()
 
     barrier = pltpu.get_barrier_semaphore()
     for s in range(1, M):
@@ -75,41 +80,39 @@
             barrier, inc=1, device_id={"dp": lax.rem(dp + s, D)}, device_id_type=MESH
         )
 
-    loads[0].wait()
-    loads[1].wait()
-
     def first(i, carry):
         fo32[pl.ds(i, B, stride=nb), :] = dot(r_v[i], a_v[i], 0, 0)
         return carry
 
-    lax.fori_loop(0, nb, first, 0, unroll=4)
-    pl.semaphore_wait(barrier, (M - 1) + (D - 1))
-
     mine = pl.multiple_of(mp * nb, nb)
-    forward = []
-    for c in range(NC):
-        step = []
-        for s in range(1, M):
-            target = lax.rem(mp + s, M)
-            base = target * nb + c * jc
-
-            def pack(j, carry, base=base):
-                at = pl.multiple_of((base + j) * nb, nb)
-                fs[base + j] = fo32[pl.ds(at, nb), :].astype(BF16)
-                return carry
-
-            lax.fori_loop(0, jc, pack, 0, unroll=4)
-            copy = remote(
-                fs.at[pl.ds(base, jc)],
-                fr.at[pl.ds(c * jc, jc), pl.ds(mine, nb)],
-                fs_sem.at[c, s - 1],
-                fr_sem.at[c, s - 1],
-                "mp",
-                target,
-            )
-            copy.start()
-            step.append(copy)
-        forward.append(step)
+    forward = [[] for _ in range(NC)]
+    for p in range(2):
+        loads[p].wait()
+        loads[2 + p].wait()
+        lax.fori_loop(p * half, (p + 1) * half, first, 0, unroll=4)
+        if p == 0:
+            pl.semaphore_wait(barrier, (M - 1) + (D - 1))
+        for c in range(NC):
+            for s in range(1, M):
+                target = lax.rem(mp + s, M)
+                base = target * nb + c * jc
+
+                def pack(j, carry, base=base, p=p):
+                    at = pl.multiple_of((base + j) * nb + p * half, half)
+                    fs[base + j, pl.ds(p * half, half), :] = fo32[pl.ds(at, half), :].astype(BF16)
+                    return carry
+
+                lax.fori_loop(0, jc, pack, 0, unroll=4)
+                copy = remote(
+                    fs.at[pl.ds(base, jc), pl.ds(p * half, half)],
+                    fr.at[pl.ds(c * jc, jc), pl.ds(pl.multiple_of(mine + p * half, half), half)],
+                    fs_sem.at[c * 2 + p, s - 1],
+                    fr_sem.at[c * 2 + p, s - 1],
+                    "mp",
+                    target,
+                )
+                copy.start()
+                forward[c].append(copy)
 
     def own(j, carry):
         at = pl.multiple_of((mine + j) * nb, nb)
@@ -117,8 +120,8 @@
         return carry
 
     lax.fori_loop(0, nb, own, 0, unroll=4)
-    loads[2].wait()
-    loads[3].wait()
+    loads[4].wait()
+    loads[5].wait()
 
     def second(jj, carry):
         x, left = fr[jj], l_v[jj]
@@ -131,43 +134,49 @@
             tl_s[d, jj] = term[d * rows : (d + 1) * rows]
         return carry
 
-    back, sums_l = [], []
-    per_half = NC // H
-    for h in range(H):
-        for c in range(h * per_half, (h + 1) * per_half):
-            for copy in forward[c]:
-                copy.wait_recv()
-            lax.fori_loop(c * jc, (c + 1) * jc, second, 0, unroll=2)
-
+    back, sums_l = [[] for _ in range(G)], []
+
+    def turn(h, g, s):
+        base = lax.rem(mp + s, M) * nb + g * ic
+
+        def one(i, carry):
+            part = gf32[pl.ds(h * hj * B + base + i, hj, stride=B), :]
+            gs[base + i, pl.ds(h * hj, hj), :] = part.astype(BF16)
+            return carry
+
+        lax.fori_loop(0, ic, one, 0, unroll=4)
+
+    def turn_own(h):
         at_j = pl.multiple_of(mine + h * hj, hj)
-        for g in range(G):
-            for s in range(1, M):
-                target = lax.rem(mp + s, M)
-                base = target * nb + g * ic
-
-                def turn(i, carry, base=base):
-                    part = gf32[pl.ds(h * hj * B + base + i, hj, stride=B), :]
-                    gs[base + i, pl.ds(h * hj, hj), :] = part.astype(BF16)
-                    return carry
-
-                lax.fori_loop(0, ic, turn, 0, unroll=4)
-                copy = remote(
-                    gs.at[pl.ds(base, ic), pl.ds(h * hj, hj)],
-                    gb.at[pl.ds(g * ic, ic), pl.ds(at_j, hj)],
-                    gs_sem.at[h * G + g, s - 1],
-                    gb_sem.at[h * G + g, s - 1],
-                    "mp",
-                    target,
-                )
-                copy.start()
-                back.append((g, copy))
-
-        def turn_own(i, carry):
+
+        def one(i, carry):
             part = gf32[pl.ds(h * hj * B + mine + i, hj, stride=B), :]
             gb[i, pl.ds(at_j, hj), :] = part.astype(BF16)
             return carry
 
-        lax.fori_loop(0, nb, turn_own, 0, unroll=4)
+        lax.fori_loop(0, nb, one, 0, unroll=4)
+
+    def send_back(h, g, s):
+        target = lax.rem(mp + s, M)
+        base = target * nb + g * ic
+        at_j = pl.multiple_of(mine + h * hj, hj)
+        copy = remote(
+            gs.at[pl.ds(base, ic), pl.ds(h * hj, hj)],
+            gb.at[pl.ds(g * ic, ic), pl.ds(at_j, hj)],
+            gs_sem.at[h * G + g, s - 1],
+            gb_sem.at[h * G + g, s - 1],
+            "mp",
+            target,
+        )
+        copy.start()
+        back[g].append(copy)
+
+    def turn_and_send(h, g):
+        for s in range(1, M):
+            turn(h, g, s)
+            send_back(h, g, s)
+
+    def send_l(h):
         for s in range(1, D):
             target = lax.rem(dp + s, D)
             copy = remote(
@@ -181,6 +190,21 @@
             copy.start()
             sums_l.append(copy)
 
+    for c in range(NC):
+        for copy in forward[c]:
+            copy.wait_recv()
+        lax.fori_loop(c * jc, (c + 1) * jc, second, 0, unroll=2)
+        if c == 1:
+            send_l(0)
+            turn_own(0)
+        if c == 2:
+            for g in range(G):
+                turn_and_send(0, g)
+    for g in range(AHEAD):
+        turn_and_send(1, g)
+    send_l(1)
+    turn_own(1)
+
     stores = [pltpu.make_async_copy(out_v, out_hbm, out_sem.at[0])]
     stores[0].start()
 
@@ -190,12 +214,6 @@
             total = total + tl_r[s, jj].astype(F32)
         gl_v[jj] = total
         return carry
-
-    for copy in sums_l:
-        copy.wait_recv()
-    lax.fori_loop(0, nb, add_l, 0, unroll=2)
-    stores.append(pltpu.make_async_copy(gl_v, gl_hbm, out_sem.at[1]))
-    stores[-1].start()
 
     def last(ii, carry):
         y = gb[ii]
@@ -207,9 +225,10 @@
 
     sums_r = []
     for g in range(G):
-        for group, copy in back:
-            if group == g:
-                copy.wait_recv()
+        for copy in back[g]:
+            copy.wait_recv()
+        if g + AHEAD < G:
+            turn_and_send(1, g + AHEAD)
         lax.fori_loop(g * ic, (g + 1) * ic, last, 0, unroll=2)
         step = []
         for s in range(1, D):
@@ -225,6 +244,12 @@
             copy.start()
             step.append(copy)
         sums_r.append(step)
+        if g == G - 3:
+            for copy in sums_l:
+                copy.wait_recv()
+            lax.fori_loop(0, nb, add_l, 0, unroll=2)
+            stores.append(pltpu.make_async_copy(gl_v, gl_hbm, out_sem.at[1]))
+            stores[-1].start()
     stores.append(pltpu.make_async_copy(gi_v, gi_hbm, out_sem.at[2]))
     stores[-1].start()
 
@@ -242,15 +267,22 @@
     stores.append(pltpu.make_async_copy(gr_v, gr_hbm, out_sem.at[3]))
     stores[-1].start()
 
-    for step in forward + sums_r:
+    for step in forward + back + sums_r:
         for copy in step:
             copy.wait_send()
-    for _, copy in back:
-        copy.wait_send()
     for copy in sums_l:
         copy.wait_send()
     for store in stores:
         store.wait()
+
+
+def write_out(*refs):
+    done = refs[8]
+    copies = [pltpu.make_async_copy(refs[n], refs[4 + n], done.at[n]) for n in range(4)]
+    for copy in copies:
+        copy.start()
+    for copy in copies:
+        copy.wait()
 
 
 def fused(M, D, inputs, cotangent, r_factor, l_factor):
@@ -262,7 +294,7 @@
     cfg = (M, D, nb, B, T, rows, scale, NC, H, G)
     sem = pltpu.SemaphoreType.DMA
     flops = 6 * 2 * nb * B * B * T
-    outputs, grad_inputs, grad_r, grad_l = pl.pallas_call(
+    results = pl.pallas_call(
         functools.partial(kernel, cfg),
         out_shape=(
             jax.ShapeDtypeStruct((nb, B, T), BF16),
@@ -270,7 +302,7 @@
             jax.ShapeDtypeStruct((nb, rows, B), F32),
             jax.ShapeDtypeStruct((nb, rows, B), F32),
         ),
-        in_specs=[pl.BlockSpec(memory_space=pl.ANY)] * 4,
+        in_specs=[pl.BlockSpec(memory_space=pltpu.HBM)] * 4,
         out_specs=[pl.BlockSpec(memory_space=pl.ANY)] * 4,
         scratch_shapes=[
             pltpu.VMEM((nb, B, T), BF16),
@@ -291,10 +323,10 @@
             pltpu.VMEM((D - 1, nb, rows, B), BF16),
             pltpu.VMEM((nb, rows, B), F32),
             pltpu.VMEM((nb, rows, B), F32),
+            sem((6,)),
             sem((4,)),
-            sem((4,)),
-            sem((NC, M - 1)),
-            sem((NC, M - 1)),
+            sem((NC * 2, M - 1)),
+            sem((NC * 2, M - 1)),
             sem((H * G, M - 1)),
             sem((H * G, M - 1)),
             sem((H, D - 1)),
@@ -303,7 +335,7 @@
             sem((G, D - 1)),
         ],
         compiler_params=pltpu.CompilerParams(
-            collective_id=0, has_side_effects=True, vmem_limit_bytes=48 * 2**20
+            collective_id=0, has_side_effects=True, vmem_limit_bytes=62 * 2**20
         ),
         cost_estimate=pl.CostEstimate(
             flops=flops, bytes_accessed=8 * nb * B * T * 2, transcendentals=nb * B * T
@@ -315,6 +347,14 @@
         r_factor[0],
         l_factor[0],
     )
+    outputs, grad_inputs, grad_r, grad_l = pl.pallas_call(
+        write_out,
+        out_shape=[jax.ShapeDtypeStruct(x.shape, x.dtype) for x in results],
+        in_specs=[pl.BlockSpec(memory_space=pl.ANY)] * 4,
+        out_specs=[pl.BlockSpec(memory_space=pltpu.HBM)] * 4,
+        scratch_shapes=[sem((4,))],
+        name="write_out",
+    )(*results)
     return (
         outputs.reshape(nb * B, T),
         grad_inputs.reshape(nb * B, T),

time: 71 us -> 147 us (2.07)
  Pallas kernels: 63.1 us -> 146 us
  local copies, waits for them, and re-layouts: 7.01 us -> 0 us
    pallas_call x0 -> x1, Pallas kernels: none -> 80.5 us  [fused(): pl.pallas_call(write_out, out_shape=[jax.ShapeDtypeStruct(x.shape, x.dtyp...]
    unnamed x10 -> x0, local copies, waits for them, and re-layouts: 7.01 us -> none
    pallas_call x1, Pallas kernels: 63.1 us -> 65.4 us  [fused(): pl.pallas_call(functools.partial(kernel, cfg), out_shape=(jax.ShapeDtypeS...]
where the time goes in v2:
time: 147 us
  Pallas kernels  146 us (99%)
    pallas_call x1, Pallas kernels, fused(): pl.pallas_call(write_out, out_shape=[jax.ShapeDtypeStruct(x.shape, x.dtyp...  80.5 us
    pallas_call x1, Pallas kernels, fused(): pl.pallas_call(functools.partial(kernel, cfg), out_shape=(jax.ShapeDtypeS...  65.4 us

profile of v2, /device:TPU:0, one launch (start us, length us, event | category | flops | bytes accessed | tf_op | source)
XLA Modules:
  0.0 146.6 jit_solution(7949153431275634878)
XLA Ops:
  0.6 65.4 %monarch.1 = (bf16[32,128,128]{2,1,0:T(8,128)(2,1)}, bf16[32,128,128]{2,1,0:T(8,128)(2,1)}, f32[32,16,128]{2,1,0:T(8,128)}, f32[32,16,128]{2,1,0:T(8,128)}) custom-call(bf16[32,128,128]{2,1,0:T(8,128)(2,1)} %bitcast.8, bf16[32,128,128]{2,1,0:T(8,128)(2,1)} %bitcast.9, bf16[32,128,128]{2,1,0:T(8,128)(2,1)} %bitcast.10, bf16[32,128,128]{2,1,0:T(8,128)(2,1)} %bitcast.11), custom_call_target="tpu_custom_call" | custom-call | flops 805306368 | bytes 8388608 | tf_op jit(solution)/shard_map/monarch/pallas_call | solution.py:297
  66.0 80.5 %write_out.1 = (bf16[32,128,128]{2,1,0:T(8,128)(2,1)}, bf16[32,128,128]{2,1,0:T(8,128)(2,1)}, f32[32,16,128]{2,1,0:T(8,128)}, f32[32,16,128]{2,1,0:T(8,128)}) custom-call(bf16[32,128,128]{2,1,0:T(8,128)(2,1)} %get-tuple-element.12.refs_0_, bf16[32,128,128]{2,1,0:T(8,128)(2,1)} %get-tuple-element.13.refs_1_, f32[32,16,128]{2,1,0:T(8,128)} %get-tuple-element.14.refs_2_, ...), custom_call_target="tpu_custom_call" | custom-call | tf_op jit(solution)/shard_map/write_out/pallas_call | solution.py:350

commit v3 on v2

--- a/solution.py
+++ b/solution.py
@@ -86,33 +86,37 @@
 
     mine = pl.multiple_of(mp * nb, nb)
     forward = [[] for _ in range(NC)]
+    def send_forward(c, start, size):
+        for s in range(1, M):
+            target = lax.rem(mp + s, M)
+            base = target * nb + c * jc
+
+            def pack(j, carry, base=base):
+                at = pl.multiple_of((base + j) * nb + start, half)
+                fs[base + j, pl.ds(start, size), :] = fo32[pl.ds(at, size), :].astype(BF16)
+                return carry
+
+            lax.fori_loop(0, jc, pack, 0, unroll=4)
+            slot = c * 2 + start // half
+            copy = remote(
+                fs.at[pl.ds(base, jc), pl.ds(start, size)],
+                fr.at[pl.ds(c * jc, jc), pl.ds(pl.multiple_of(mine + start, half), size)],
+                fs_sem.at[slot, s - 1],
+                fr_sem.at[slot, s - 1],
+                "mp",
+                target,
+            )
+            copy.start()
+            forward[c].append(copy)
+
     for p in range(2):
         loads[p].wait()
         loads[2 + p].wait()
         lax.fori_loop(p * half, (p + 1) * half, first, 0, unroll=4)
         if p == 0:
             pl.semaphore_wait(barrier, (M - 1) + (D - 1))
-        for c in range(NC):
-            for s in range(1, M):
-                target = lax.rem(mp + s, M)
-                base = target * nb + c * jc
-
-                def pack(j, carry, base=base, p=p):
-                    at = pl.multiple_of((base + j) * nb + p * half, half)
-                    fs[base + j, pl.ds(p * half, half), :] = fo32[pl.ds(at, half), :].astype(BF16)
-                    return carry
-
-                lax.fori_loop(0, jc, pack, 0, unroll=4)
-                copy = remote(
-                    fs.at[pl.ds(base, jc), pl.ds(p * half, half)],
-                    fr.at[pl.ds(c * jc, jc), pl.ds(pl.multiple_of(mine + p * half, half), half)],
-                    fs_sem.at[c * 2 + p, s - 1],
-                    fr_sem.at[c * 2 + p, s - 1],
-                    "mp",
-                    target,
-                )
-                copy.start()
-                forward[c].append(copy)
+        for c in range(AHEAD):
+            send_forward(c, p * half, half)
 
     def own(j, carry):
         at = pl.multiple_of((mine + j) * nb, nb)
@@ -193,13 +197,16 @@
     for c in range(NC):
         for copy in forward[c]:
             copy.wait_recv()
+        if c + AHEAD < NC:
+            send_forward(c + AHEAD, 0, nb)
+        else:
+            first_group = (c + AHEAD - NC) * (G // AHEAD)
+            for g in range(first_group, first_group + G // AHEAD):
+                turn_and_send(0, g)
         lax.fori_loop(c * jc, (c + 1) * jc, second, 0, unroll=2)
         if c == 1:
             send_l(0)
             turn_own(0)
-        if c == 2:
-            for g in range(G):
-                turn_and_send(0, g)
     for g in range(AHEAD):
         turn_and_send(1, g)
     send_l(1)
@@ -277,12 +284,24 @@
 
 
 def write_out(*refs):
-    done = refs[8]
-    copies = [pltpu.make_async_copy(refs[n], refs[4 + n], done.at[n]) for n in range(4)]
-    for copy in copies:
-        copy.start()
-    for copy in copies:
-        copy.wait()
+    sources, results, held, (in_sem, out_sem) = refs[:4], refs[4:8], refs[8:12], refs[12:]
+    pieces = []
+    for src, mid, dst, parts in zip(sources, held, results, (2, 2, 1, 1)):
+        size = src.shape[0] // parts
+        for p in range(parts):
+            at = pl.ds(p * size, size)
+            n = len(pieces)
+            pieces.append((
+                pltpu.make_async_copy(src.at[at], mid.at[at], in_sem.at[n]),
+                pltpu.make_async_copy(mid.at[at], dst.at[at], out_sem.at[n]),
+            ))
+    for load, _ in pieces:
+        load.start()
+    for load, store in pieces:
+        load.wait()
+        store.start()
+    for _, store in pieces:
+        store.wait()
 
 
 def fused(M, D, inputs, cotangent, r_factor, l_factor):
@@ -352,7 +371,8 @@
         out_shape=[jax.ShapeDtypeStruct(x.shape, x.dtype) for x in results],
         in_specs=[pl.BlockSpec(memory_space=pl.ANY)] * 4,
         out_specs=[pl.BlockSpec(memory_space=pltpu.HBM)] * 4,
-        scratch_shapes=[sem((4,))],
+        scratch_shapes=[pltpu.VMEM(x.shape, x.dtype) for x in results] + [sem((6,)), sem((6,))],
+        compiler_params=pltpu.CompilerParams(vmem_limit_bytes=62 * 2**20),
         name="write_out",
     )(*results)
     return (

time: 147 us -> 64.2 us (0.44)
  Pallas kernels: 146 us -> 63.4 us
    pallas_call x1, Pallas kernels: 80.5 us -> 2.63 us  [fused(): pl.pallas_call(write_out, out_shape=[jax.ShapeDtypeStruct(x.shape, x.dtyp...]
    pallas_call x1, Pallas kernels: 65.4 us -> 60.8 us  [fused(): pl.pallas_call(functools.partial(kernel, cfg), out_shape=(jax.ShapeDtypeS...]
where the time goes in v3:
time: 64.2 us; the launch traced here: 64 us
  Pallas kernels  63.4 us (99%)
    pallas_call x1, Pallas kernels, fused(): pl.pallas_call(functools.partial(kernel, cfg), out_shape=(jax.ShapeDtypeS...  60.8 us
    pallas_call x1, Pallas kernels, fused(): pl.pallas_call(write_out, out_shape=[jax.ShapeDtypeStruct(x.shape, x.dtyp...  2.63 us

profile of v3, /device:TPU:0, one launch (start us, length us, event | category | flops | bytes accessed | tf_op | source)
XLA Modules:
  0.0 64.0 jit_solution(3468722639826940092)
XLA Ops:
  0.6 60.8 %monarch.1 = (bf16[32,128,128]{2,1,0:T(8,128)(2,1)}, bf16[32,128,128]{2,1,0:T(8,128)(2,1)}, f32[32,16,128]{2,1,0:T(8,128)}, f32[32,16,128]{2,1,0:T(8,128)}) custom-call(bf16[32,128,128]{2,1,0:T(8,128)(2,1)} %bitcast.8, bf16[32,128,128]{2,1,0:T(8,128)(2,1)} %bitcast.9, bf16[32,128,128]{2,1,0:T(8,128)(2,1)} %bitcast.10, bf16[32,128,128]{2,1,0:T(8,128)(2,1)} %bitcast.11), custom_call_target="tpu_custom_call" | custom-call | flops 805306368 | bytes 8388608 | tf_op jit(solution)/shard_map/monarch/pallas_call | solution.py:316
  61.4 2.6 %write_out.1 = (bf16[32,128,128]{2,1,0:T(8,128)(2,1)}, bf16[32,128,128]{2,1,0:T(8,128)(2,1)}, f32[32,16,128]{2,1,0:T(8,128)}, f32[32,16,128]{2,1,0:T(8,128)}) custom-call(bf16[32,128,128]{2,1,0:T(8,128)(2,1)} %get-tuple-element.12.refs_0_, bf16[32,128,128]{2,1,0:T(8,128)(2,1)} %get-tuple-element.13.refs_1_, f32[32,16,128]{2,1,0:T(8,128)} %get-tuple-element.14.refs_2_, ...), custom_call_target="tpu_custom_call" | custom-call | tf_op jit(solution)/shard_map/write_out/pallas_call | solution.py:369

commit v4 on v3

--- a/solution.py
+++ b/solution.py
@@ -47,14 +47,14 @@
     fo32, fs, fr,
     gf32, gs, gb,
     out_v, gi_v,
-    tl_s, tl_r, tr_s, tr_r,
+    tl_s, tl_r, tr_s, tr_p, tr_c, tr_r,
     gl_v, gr_v,
     in_sem, out_sem,
     fs_sem, fr_sem, gs_sem, gb_sem,
-    ls_sem, lr_sem, rs_sem, rr_sem,
+    ls_sem, lr_sem, ps_sem, pr_sem, rs_sem, rr_sem,
 ):
-    M, D, nb, B, T, rows, scale, NC, H, G = cfg
-    jc, hj, ic = nb // NC, nb // H, nb // G
+    M, D, nb, B, T, rows, scale, NC, H, GROUPS = cfg
+    jc, hj = nb // NC, nb // H
     mp, dp = lax.axis_index("mp"), lax.axis_index("dp")
 
     half = nb // 2
@@ -138,17 +138,17 @@
             tl_s[d, jj] = term[d * rows : (d + 1) * rows]
         return carry
 
-    back, sums_l = [[] for _ in range(G)], []
-
-    def turn(h, g, s):
-        base = lax.rem(mp + s, M) * nb + g * ic
+    back, sums_l = [[] for _ in range(len(GROUPS))], []
+
+    def turn(h, start, size, s):
+        base = lax.rem(mp + s, M) * nb + start
 
         def one(i, carry):
             part = gf32[pl.ds(h * hj * B + base + i, hj, stride=B), :]
             gs[base + i, pl.ds(h * hj, hj), :] = part.astype(BF16)
             return carry
 
-        lax.fori_loop(0, ic, one, 0, unroll=4)
+        lax.fori_loop(0, size, one, 0, unroll=4)
 
     def turn_own(h):
         at_j = pl.multiple_of(mine + h * hj, hj)
@@ -160,25 +160,22 @@
 
         lax.fori_loop(0, nb, one, 0, unroll=4)
 
-    def send_back(h, g, s):
-        target = lax.rem(mp + s, M)
-        base = target * nb + g * ic
-        at_j = pl.multiple_of(mine + h * hj, hj)
-        copy = remote(
-            gs.at[pl.ds(base, ic), pl.ds(h * hj, hj)],
-            gb.at[pl.ds(g * ic, ic), pl.ds(at_j, hj)],
-            gs_sem.at[h * G + g, s - 1],
-            gb_sem.at[h * G + g, s - 1],
-            "mp",
-            target,
-        )
-        copy.start()
-        back[g].append(copy)
-
-    def turn_and_send(h, g):
+    def turn_and_send(n):
+        h, start, size = GROUPS[n]
         for s in range(1, M):
-            turn(h, g, s)
-            send_back(h, g, s)
+            turn(h, start, size, s)
+            target = lax.rem(mp + s, M)
+            at_j = pl.multiple_of(mine + h * hj, hj)
+            copy = remote(
+                gs.at[pl.ds(target * nb + start, size), pl.ds(h * hj, hj)],
+                gb.at[pl.ds(start, size), pl.ds(at_j, hj)],
+                gs_sem.at[n, s - 1],
+                gb_sem.at[n, s - 1],
+                "mp",
+                target,
+            )
+            copy.start()
+            back[n].append(copy)
 
     def send_l(h):
         for s in range(1, D):
@@ -200,15 +197,13 @@
         if c + AHEAD < NC:
             send_forward(c + AHEAD, 0, nb)
         else:
-            first_group = (c + AHEAD - NC) * (G // AHEAD)
-            for g in range(first_group, first_group + G // AHEAD):
-                turn_and_send(0, g)
+            turn_and_send(c + AHEAD - NC)
         lax.fori_loop(c * jc, (c + 1) * jc, second, 0, unroll=2)
         if c == 1:
             send_l(0)
             turn_own(0)
-    for g in range(AHEAD):
-        turn_and_send(1, g)
+    for n in range(AHEAD):
+        turn_and_send(AHEAD + n)
     send_l(1)
     turn_own(1)
 
@@ -222,62 +217,102 @@
         gl_v[jj] = total
         return carry
 
+    chip, core = lax.div(dp, 2), lax.rem(dp, 2)
+    chips = D // 2
+
     def last(ii, carry):
         y = gb[ii]
         gi_v[ii] = dot(r_v[ii], y, 1, 0).astype(BF16)
         term = (dot(a_v[ii], y, 1, 1) * scale).astype(BF16)
         for d in range(D):
-            tr_s[d, ii] = term[d * rows : (d + 1) * rows]
-        return carry
-
-    sums_r = []
-    for g in range(G):
-        for copy in back[g]:
-            copy.wait_recv()
-        if g + AHEAD < G:
-            turn_and_send(1, g + AHEAD)
-        lax.fori_loop(g * ic, (g + 1) * ic, last, 0, unroll=2)
+            tr_s[d % 2, d // 2, ii] = term[d * rows : (d + 1) * rows]
+        return carry
+
+    def pair_sum(q, ii):
+        return tr_s[core, q, ii].astype(F32) + tr_p[q, ii].astype(F32)
+
+    pairs, sums_r = [], []
+
+    def send_pair(g):
+        at = pl.ds(*GROUPS[AHEAD + g][1:])
+        copy = remote(
+            tr_s.at[1 - core, :, at], tr_p.at[:, at], ps_sem.at[g], pr_sem.at[g],
+            "dp", dp + 1 - 2 * core,
+        )
+        copy.start()
+        pairs.append(copy)
+
+    def send_chips(g):
+        start, size = GROUPS[AHEAD + g][1:]
+        pairs[g].wait_recv()
         step = []
-        for s in range(1, D):
-            target = lax.rem(dp + s, D)
+        for s in range(1, chips):
+            q = lax.rem(chip + s, chips)
+
+            def add(ii, carry, q=q):
+                tr_c[q, ii] = pair_sum(q, ii).astype(BF16)
+                return carry
+
+            lax.fori_loop(start, start + size, add, 0, unroll=4)
             copy = remote(
-                tr_s.at[target, pl.ds(g * ic, ic)],
-                tr_r.at[s - 1, pl.ds(g * ic, ic)],
+                tr_c.at[q, pl.ds(start, size)],
+                tr_r.at[s - 1, pl.ds(start, size)],
                 rs_sem.at[g, s - 1],
                 rr_sem.at[g, s - 1],
                 "dp",
-                target,
+                2 * q + core,
             )
             copy.start()
             step.append(copy)
         sums_r.append(step)
-        if g == G - 3:
+
+    def add_r(ii, carry):
+        total = pair_sum(chip, ii)
+        for s in range(chips - 1):
+            total = total + tr_r[s, ii].astype(F32)
+        gr_v[ii] = total
+        return carry
+
+    def finish(g):
+        start, size = GROUPS[AHEAD + g][1:]
+        for copy in sums_r[g]:
+            copy.wait_recv()
+        lax.fori_loop(start, start + size, add_r, 0, unroll=4)
+
+    count = len(GROUPS) - AHEAD
+    for g in range(count):
+        start, size = GROUPS[AHEAD + g][1:]
+        for n in range(AHEAD):
+            if GROUPS[n][1] == start:
+                for copy in back[n]:
+                    copy.wait_recv()
+        for copy in back[AHEAD + g]:
+            copy.wait_recv()
+        if g + AHEAD < count:
+            turn_and_send(g + 2 * AHEAD)
+        lax.fori_loop(start, start + size, last, 0, unroll=2)
+        send_pair(g)
+        at = pl.ds(start, size)
+        stores.append(pltpu.make_async_copy(gi_v.at[at], gi_hbm.at[at], out_sem.at[3 + g]))
+        stores[-1].start()
+        if g >= 1:
+            send_chips(g - 1)
+        if g == 1:
             for copy in sums_l:
                 copy.wait_recv()
             lax.fori_loop(0, nb, add_l, 0, unroll=2)
             stores.append(pltpu.make_async_copy(gl_v, gl_hbm, out_sem.at[1]))
             stores[-1].start()
-    stores.append(pltpu.make_async_copy(gi_v, gi_hbm, out_sem.at[2]))
-    stores[-1].start()
-
-    def add_r(ii, carry):
-        total = tr_s[dp, ii].astype(F32)
-        for s in range(D - 1):
-            total = total + tr_r[s, ii].astype(F32)
-        gr_v[ii] = total
-        return carry
-
-    for g in range(G):
-        for copy in sums_r[g]:
-            copy.wait_recv()
-        lax.fori_loop(g * ic, (g + 1) * ic, add_r, 0, unroll=2)
-    stores.append(pltpu.make_async_copy(gr_v, gr_hbm, out_sem.at[3]))
+    send_chips(count - 1)
+    for g in range(count):
+        finish(g)
+    stores.append(pltpu.make_async_copy(gr_v, gr_hbm, out_sem.at[2]))
     stores[-1].start()
 
     for step in forward + back + sums_r:
         for copy in step:
             copy.wait_send()
-    for copy in sums_l:
+    for copy in sums_l + pairs:
         copy.wait_send()
     for store in stores:
         store.wait()
@@ -309,8 +344,13 @@
     T = inputs.shape[1]
     rows = B // D
     scale = float(D * T) ** (-0.5)
-    NC, H, G = 4, 2, 4
-    cfg = (M, D, nb, B, T, rows, scale, NC, H, G)
+    NC, H = 4, 2
+    half, part, small = nb // 2, nb // 4, nb // 8
+    groups = ((0, 0, half), (0, half, half))
+    groups += ((1, 0, part), (1, part, part), (1, half, part))
+    groups += ((1, half + part, small), (1, half + part + small, small))
+    cfg = (M, D, nb, B, T, rows, scale, NC, H, groups)
+    count = len(groups) - AHEAD
     sem = pltpu.SemaphoreType.DMA
     flops = 6 * 2 * nb * B * B * T
     results = pl.pallas_call(
@@ -338,20 +378,24 @@
             pltpu.VMEM((nb, B, T), BF16),
             pltpu.VMEM((D, nb, rows, B), BF16),
             pltpu.VMEM((D - 1, nb, rows, B), BF16),
-            pltpu.VMEM((D, nb, rows, B), BF16),
-            pltpu.VMEM((D - 1, nb, rows, B), BF16),
+            pltpu.VMEM((2, D // 2, nb, rows, B), BF16),
+            pltpu.VMEM((D // 2, nb, rows, B), BF16),
+            pltpu.VMEM((D // 2, nb, rows, B), BF16),
+            pltpu.VMEM((D // 2 - 1, nb, rows, B), BF16),
             pltpu.VMEM((nb, rows, B), F32),
             pltpu.VMEM((nb, rows, B), F32),
             sem((6,)),
-            sem((4,)),
+            sem((3 + count,)),
             sem((NC * 2, M - 1)),
             sem((NC * 2, M - 1)),
-            sem((H * G, M - 1)),
-            sem((H * G, M - 1)),
+            sem((len(groups), M - 1)),
+            sem((len(groups), M - 1)),
             sem((H, D - 1)),
             sem((H, D - 1)),
-            sem((G, D - 1)),
-            sem((G, D - 1)),
+            sem((count,)),
+            sem((count,)),
+            sem((count, D // 2 - 1)),
+            sem((count, D // 2 - 1)),
         ],
         compiler_params=pltpu.CompilerParams(
             collective_id=0, has_side_effects=True, vmem_limit_bytes=62 * 2**20
@@ -418,7 +462,7 @@
 
     def shards(inputs, cotangent, r_factor, l_factor):
         nb, B = r_factor.shape[1], r_factor.shape[2]
-        tiled = nb % 32 == 0 and (B // D) % 16 == 0 and M > 1 and D > 1
+        tiled = nb % 32 == 0 and (B // D) % 16 == 0 and M > 1 and D > 2 and D % 2 == 0
         return (fused if tiled else plain)(M, D, inputs, cotangent, r_factor, l_factor)
 
     return jax.shard_map(

time: 64.2 us -> 64.4 us (level)
  no operation moved by 1% of the time
where the time goes in v4:
time: 64.4 us; the launch traced here: 64.3 us
  Pallas kernels  63.6 us (99%)
    pallas_call x1, Pallas kernels, fused(): pl.pallas_call(functools.partial(kernel, cfg), out_shape=(jax.ShapeDtypeS...  61 us
    pallas_call x1, Pallas kernels, fused(): pl.pallas_call(write_out, out_shape=[jax.ShapeDtypeStruct(x.shape, x.dtyp...  2.63 us

profile of v4, /device:TPU:0, one launch (start us, length us, event | category | flops | bytes accessed | tf_op | source)
XLA Modules:
  0.0 64.3 jit_solution(9654322208180630496)
XLA Ops:
  0.6 61.0 %monarch.1 = (bf16[32,128,128]{2,1,0:T(8,128)(2,1)}, bf16[32,128,128]{2,1,0:T(8,128)(2,1)}, f32[32,16,128]{2,1,0:T(8,128)}, f32[32,16,128]{2,1,0:T(8,128)}) custom-call(bf16[32,128,128]{2,1,0:T(8,128)(2,1)} %bitcast.8, bf16[32,128,128]{2,1,0:T(8,128)(2,1)} %bitcast.9, bf16[32,128,128]{2,1,0:T(8,128)(2,1)} %bitcast.10, bf16[32,128,128]{2,1,0:T(8,128)(2,1)} %bitcast.11), custom_call_target="tpu_custom_call" | custom-call | flops 805306368 | bytes 8388608 | tf_op jit(solution)/shard_map/monarch/pallas_call | solution.py:356
  61.6 2.6 %write_out.1 = (bf16[32,128,128]{2,1,0:T(8,128)(2,1)}, bf16[32,128,128]{2,1,0:T(8,128)(2,1)}, f32[32,16,128]{2,1,0:T(8,128)}, f32[32,16,128]{2,1,0:T(8,128)}) custom-call(bf16[32,128,128]{2,1,0:T(8,128)(2,1)} %get-tuple-element.12.refs_0_, bf16[32,128,128]{2,1,0:T(8,128)(2,1)} %get-tuple-element.13.refs_1_, f32[32,16,128]{2,1,0:T(8,128)} %get-tuple-element.14.refs_2_, ...), custom_call_target="tpu_custom_call" | custom-call | tf_op jit(solution)/shard_map/write_out/pallas_call | solution.py:413

commit v5 on v4

--- a/solution.py
+++ b/solution.py
@@ -42,16 +42,14 @@
 def kernel(
     cfg,
     a_hbm, g_hbm, r_hbm, l_hbm,
-    out_hbm, gi_hbm, gr_hbm, gl_hbm,
+    out_v, gi_v, gr_v, gl_v,
     a_v, g_v, r_v, l_v,
     fo32, fs, fr,
     gf32, gs, gb,
-    out_v, gi_v,
-    tl_s, tl_r, tr_s, tr_p, tr_c, tr_r,
-    gl_v, gr_v,
-    in_sem, out_sem,
+    tl_s, tl_r, tr_s, tr_r,
+    in_sem,
     fs_sem, fr_sem, gs_sem, gb_sem,
-    ls_sem, lr_sem, ps_sem, pr_sem, rs_sem, rr_sem,
+    ls_sem, lr_sem, rs_sem, rr_sem,
 ):
     M, D, nb, B, T, rows, scale, NC, H, GROUPS = cfg
     jc, hj = nb // NC, nb // H
@@ -207,9 +205,6 @@
     send_l(1)
     turn_own(1)
 
-    stores = [pltpu.make_async_copy(out_v, out_hbm, out_sem.at[0])]
-    stores[0].start()
-
     def add_l(jj, carry):
         total = tl_s[dp, jj].astype(F32)
         for s in range(D - 1):
@@ -217,58 +212,36 @@
         gl_v[jj] = total
         return carry
 
-    chip, core = lax.div(dp, 2), lax.rem(dp, 2)
-    chips = D // 2
-
     def last(ii, carry):
         y = gb[ii]
         gi_v[ii] = dot(r_v[ii], y, 1, 0).astype(BF16)
         term = (dot(a_v[ii], y, 1, 1) * scale).astype(BF16)
         for d in range(D):
-            tr_s[d % 2, d // 2, ii] = term[d * rows : (d + 1) * rows]
-        return carry
-
-    def pair_sum(q, ii):
-        return tr_s[core, q, ii].astype(F32) + tr_p[q, ii].astype(F32)
-
-    pairs, sums_r = [], []
-
-    def send_pair(g):
+            tr_s[d, ii] = term[d * rows : (d + 1) * rows]
+        return carry
+
+    sums_r = []
+
+    def send_r(g):
         at = pl.ds(*GROUPS[AHEAD + g][1:])
-        copy = remote(
-            tr_s.at[1 - core, :, at], tr_p.at[:, at], ps_sem.at[g], pr_sem.at[g],
-            "dp", dp + 1 - 2 * core,
-        )
-        copy.start()
-        pairs.append(copy)
-
-    def send_chips(g):
-        start, size = GROUPS[AHEAD + g][1:]
-        pairs[g].wait_recv()
         step = []
-        for s in range(1, chips):
-            q = lax.rem(chip + s, chips)
-
-            def add(ii, carry, q=q):
-                tr_c[q, ii] = pair_sum(q, ii).astype(BF16)
-                return carry
-
-            lax.fori_loop(start, start + size, add, 0, unroll=4)
+        for s in range(1, D):
+            target = lax.rem(dp + s, D)
             copy = remote(
-                tr_c.at[q, pl.ds(start, size)],
-                tr_r.at[s - 1, pl.ds(start, size)],
+                tr_s.at[target, at],
+                tr_r.at[s - 1, at],
                 rs_sem.at[g, s - 1],
                 rr_sem.at[g, s - 1],
                 "dp",
-                2 * q + core,
+                target,
             )
             copy.start()
             step.append(copy)
         sums_r.append(step)
 
     def add_r(ii, carry):
-        total = pair_sum(chip, ii)
-        for s in range(chips - 1):
+        total = tr_s[dp, ii].astype(F32)
+        for s in range(D - 1):
             total = total + tr_r[s, ii].astype(F32)
         gr_v[ii] = total
         return carry
@@ -291,52 +264,28 @@
         if g + AHEAD < count:
             turn_and_send(g + 2 * AHEAD)
         lax.fori_loop(start, start + size, last, 0, unroll=2)
-        send_pair(g)
-        at = pl.ds(start, size)
-        stores.append(pltpu.make_async_copy(gi_v.at[at], gi_hbm.at[at], out_sem.at[3 + g]))
-        stores[-1].start()
-        if g >= 1:
-            send_chips(g - 1)
+        send_r(g)
         if g == 1:
             for copy in sums_l:
                 copy.wait_recv()
             lax.fori_loop(0, nb, add_l, 0, unroll=2)
-            stores.append(pltpu.make_async_copy(gl_v, gl_hbm, out_sem.at[1]))
-            stores[-1].start()
-    send_chips(count - 1)
     for g in range(count):
         finish(g)
-    stores.append(pltpu.make_async_copy(gr_v, gr_hbm, out_sem.at[2]))
-    stores[-1].start()
 
     for step in forward + back + sums_r:
         for copy in step:
             copy.wait_send()
-    for copy in sums_l + pairs:
+    for copy in sums_l:
         copy.wait_send()
-    for store in stores:
-        store.wait()
 
 
 def write_out(*refs):
-    sources, results, held, (in_sem, out_sem) = refs[:4], refs[4:8], refs[8:12], refs[12:]
-    pieces = []
-    for src, mid, dst, parts in zip(sources, held, results, (2, 2, 1, 1)):
-        size = src.shape[0] // parts
-        for p in range(parts):
-            at = pl.ds(p * size, size)
-            n = len(pieces)
-            pieces.append((
-                pltpu.make_async_copy(src.at[at], mid.at[at], in_sem.at[n]),
-                pltpu.make_async_copy(mid.at[at], dst.at[at], out_sem.at[n]),
-            ))
-    for load, _ in pieces:
-        load.start()
-    for load, store in pieces:
-        load.wait()
-        store.start()
-    for _, store in pieces:
-        store.wait()
+    done = refs[8]
+    copies = [pltpu.make_async_copy(refs[n], refs[4 + n], done.at[n]) for n in range(4)]
+    for copy in copies:
+        copy.start()
+    for copy in copies:
+        copy.wait()
 
 
 def fused(M, D, inputs, cotangent, r_factor, l_factor):
@@ -356,13 +305,13 @@
     results = pl.pallas_call(
         functools.partial(kernel, cfg),
         out_shape=(
-            jax.ShapeDtypeStruct((nb, B, T), BF16),
-            jax.ShapeDtypeStruct((nb, B, T), BF16),
-            jax.ShapeDtypeStruct((nb, rows, B), F32),
-            jax.ShapeDtypeStruct((nb, rows, B), F32),
+            pltpu.VMEM((nb, B, T), BF16),
+            pltpu.VMEM((nb, B, T), BF16),
+            pltpu.VMEM((nb, rows, B), F32),
+            pltpu.VMEM((nb, rows, B), F32),
         ),
         in_specs=[pl.BlockSpec(memory_space=pltpu.HBM)] * 4,
-        out_specs=[pl.BlockSpec(memory_space=pl.ANY)] * 4,
+        out_specs=[pl.BlockSpec(memory_space=pltpu.VMEM)] * 4,
         scratch_shapes=[
             pltpu.VMEM((nb, B, T), BF16),
             pltpu.VMEM((nb, B, T), BF16),
@@ -374,31 +323,22 @@
             pltpu.VMEM((nb * B, T), F32),
             pltpu.VMEM((B, nb, T), BF16),
             pltpu.VMEM((nb, B, T), BF16),
-            pltpu.VMEM((nb, B, T), BF16),
-            pltpu.VMEM((nb, B, T), BF16),
             pltpu.VMEM((D, nb, rows, B), BF16),
             pltpu.VMEM((D - 1, nb, rows, B), BF16),
-            pltpu.VMEM((2, D // 2, nb, rows, B), BF16),
-            pltpu.VMEM((D // 2, nb, rows, B), BF16),
-            pltpu.VMEM((D // 2, nb, rows, B), BF16),
-            pltpu.VMEM((D // 2 - 1, nb, rows, B), BF16),
-            pltpu.VMEM((nb, rows, B), F32),
-            pltpu.VMEM((nb, rows, B), F32),
+            pltpu.VMEM((D, nb, rows, B), BF16),
+            pltpu.VMEM((D - 1, nb, rows, B), BF16),
             sem((6,)),
-            sem((3 + count,)),
             sem((NC * 2, M - 1)),
             sem((NC * 2, M - 1)),
             sem((len(groups), M - 1)),
             sem((len(groups), M - 1)),
             sem((H, D - 1)),
             sem((H, D - 1)),
-            sem((count,)),
-            sem((count,)),
-            sem((count, D // 2 - 1)),
-            sem((count, D // 2 - 1)),
+            sem((count, D - 1)),
+            sem((count, D - 1)),
         ],
         compiler_params=pltpu.CompilerParams(
-            collective_id=0, has_side_effects=True, vmem_limit_bytes=62 * 2**20
+            collective_id=0, has_side_effects=True, vmem_limit_bytes=61 * 2**20
         ),
         cost_estimate=pl.CostEstimate(
             flops=flops, bytes_accessed=8 * nb * B * T * 2, transcendentals=nb * B * T
@@ -413,10 +353,9 @@
     outputs, grad_inputs, grad_r, grad_l = pl.pallas_call(
         write_out,
         out_shape=[jax.ShapeDtypeStruct(x.shape, x.dtype) for x in results],
-        in_specs=[pl.BlockSpec(memory_space=pl.ANY)] * 4,
+        in_specs=[pl.BlockSpec(memory_space=pltpu.VMEM)] * 4,
         out_specs=[pl.BlockSpec(memory_space=pltpu.HBM)] * 4,
-        scratch_shapes=[pltpu.VMEM(x.shape, x.dtype) for x in results] + [sem((6,)), sem((6,))],
-        compiler_params=pltpu.CompilerParams(vmem_limit_bytes=62 * 2**20),
+        scratch_shapes=[sem((4,))],
         name="write_out",
     )(*results)
     return (
@@ -462,7 +401,7 @@
 
     def shards(inputs, cotangent, r_factor, l_factor):
         nb, B = r_factor.shape[1], r_factor.shape[2]
-        tiled = nb % 32 == 0 and (B // D) % 16 == 0 and M > 1 and D > 2 and D % 2 == 0
+        tiled = nb % 32 == 0 and (B // D) % 16 == 0 and M > 1 and D > 1
         return (fused if tiled else plain)(M, D, inputs, cotangent, r_factor, l_factor)
 
     return jax.shard_map(

time: 64.4 us -> 68 us (1.056)
  local copies, waits for them, and re-layouts: 0 us -> 3.39 us
    unnamed x0 -> x8, local copies, waits for them, and re-layouts: none -> 3.39 us
where the time goes in v5:
time: 68 us; the launch traced here: 67.8 us
  Pallas kernels  63.8 us (94%)
  local copies, waits for them, and re-layouts  3.39 us (5%)
    pallas_call x1, Pallas kernels, fused(): pl.pallas_call(functools.partial(kernel, cfg), out_shape=(pltpu.VMEM((nb,...  60.6 us
    unnamed x8, local copies, waits for them, and re-layouts  3.39 us
    pallas_call x1, Pallas kernels, fused(): pl.pallas_call(write_out, out_shape=[jax.ShapeDtypeStruct(x.shape, x.dtyp...  3.17 us

profile of v5, /device:TPU:0, one launch (start us, length us, event | category | flops | bytes accessed | tf_op | source)
XLA Modules:
  0.0 67.8 jit_solution(8363620856493128279)
XLA Ops:
  0.6 60.6 %monarch.1 = (bf16[32,128,128]{2,1,0:T(8,128)(2,1)S(1)}, bf16[32,128,128]{2,1,0:T(8,128)(2,1)S(1)}, f32[32,16,128]{2,1,0:T(8,128)S(1)}, f32[32,16,128]{2,1,0:T(8,128)S(1)}) custom-call(bf16[32,128,128]{2,1,0:T(8,128)(2,1)} %bitcast.8, bf16[32,128,128]{2,1,0:T(8,128)(2,1)} %bitcast.9, bf16[32,128,128]{2,1,0:T(8,128)(2,1)} %bitcast.10, ...), custom_call_target="tpu_custom_call" | custom-call | flops 805306368 | bytes 8388608 | tf_op jit(solution)/shard_map/monarch/pallas_call | solution.py:305
  61.3 0.0 copy-start
  61.3 1.0 %copy-done = bf16[32,128,128]{2,1,0:T(8,128)(2,1)} copy-done((bf16[32,128,128]{2,1,0:T(8,128)(2,1)}, bf16[32,128,128]{2,1,0:T(8,128)(2,1)S(1)}, u32[]{:S(2)}) %copy-start) | copy-done | bytes 1048600
  62.2 0.0 copy-start.1
  62.2 1.0 %copy-done.1 = bf16[32,128,128]{2,1,0:T(8,128)(2,1)} copy-done((bf16[32,128,128]{2,1,0:T(8,128)(2,1)}, bf16[32,128,128]{2,1,0:T(8,128)(2,1)S(1)}, u32[]{:S(2)}) %copy-start.1) | copy-done | bytes 1048600
  63.3 0.0 copy-start.2
  63.3 0.7 %copy-done.2 = f32[32,16,128]{2,1,0:T(8,128)} copy-done((f32[32,16,128]{2,1,0:T(8,128)}, f32[32,16,128]{2,1,0:T(8,128)S(1)}, u32[]{:S(2)}) %copy-start.2) | copy-done | bytes 262168
  64.0 0.0 copy-start.3
  64.0 0.7 %copy-done.3 = f32[32,16,128]{2,1,0:T(8,128)} copy-done((f32[32,16,128]{2,1,0:T(8,128)}, f32[32,16,128]{2,1,0:T(8,128)S(1)}, u32[]{:S(2)}) %copy-start.3) | copy-done | bytes 262168
  64.7 3.2 %write_out.1 = (bf16[32,128,128]{2,1,0:T(8,128)(2,1)}, bf16[32,128,128]{2,1,0:T(8,128)(2,1)}, f32[32,16,128]{2,1,0:T(8,128)}, f32[32,16,128]{2,1,0:T(8,128)}) custom-call(bf16[32,128,128]{2,1,0:T(8,128)(2,1)} %copy-done, bf16[32,128,128]{2,1,0:T(8,128)(2,1)} %copy-done.1, f32[32,16,128]{2,1,0:T(8,128)} %copy-done.2, f32[32,16,128]{2,1,0:T(8,128)} %copy-done.3), custom_call_target="tpu_custom_call" | custom-call | tf_op jit(solution)/shard_map/write_out/pallas_call | solution.py:353
Async XLA Ops:
  61.3 1.0 %copy-start = (bf16[32,128,128]{2,1,0:T(8,128)(2,1)}, bf16[32,128,128]{2,1,0:T(8,128)(2,1)S(1)}, u32[]{:S(2)}) copy-start(bf16[32,128,128]{2,1,0:T(8,128)(2,1)S(1)} %get-tuple-element.12.refs_0_) | copy-start | bytes 3145732
  62.2 1.0 %copy-start.1 = (bf16[32,128,128]{2,1,0:T(8,128)(2,1)}, bf16[32,128,128]{2,1,0:T(8,128)(2,1)S(1)}, u32[]{:S(2)}) copy-start(bf16[32,128,128]{2,1,0:T(8,128)(2,1)S(1)} %get-tuple-element.13.refs_1_) | copy-start | bytes 3145732
  63.3 0.7 %copy-start.2 = (f32[32,16,128]{2,1,0:T(8,128)}, f32[32,16,128]{2,1,0:T(8,128)S(1)}, u32[]{:S(2)}) copy-start(f32[32,16,128]{2,1,0:T(8,128)S(1)} %get-tuple-element.14.refs_2_) | copy-start | bytes 786436
  64.0 0.7 %copy-start.3 = (f32[32,16,128]{2,1,0:T(8,128)}, f32[32,16,128]{2,1,0:T(8,128)S(1)}, u32[]{:S(2)}) copy-start(f32[32,16,128]{2,1,0:T(8,128)S(1)} %get-tuple-element.15.refs_3_) | copy-start | bytes 786436

commit v6 on v5

--- a/solution.py
+++ b/solution.py
@@ -10,7 +10,8 @@
 MESH = pl.DeviceIdType.MESH
 F32 = jnp.float32
 BF16 = jnp.bfloat16
-AHEAD = 2
+AHEAD = 3
+BACK = 2
 
 
 def dot(left, right, left_dim, right_dim):
@@ -26,6 +27,12 @@
     half = 0.5 + 0.5 * tanh
     slope = half + 0.5 * v * (1.0 - tanh * tanh) * (c0 + (3.0 * c0 * c1) * square)
     return v * half, slope
+
+
+def partners(me, size):
+    if size == 4:
+        return [lax.rem(me + 2, 4), 3 - me, me + 1 - 2 * lax.rem(me, 2)]
+    return [lax.rem(me + s, size) for s in range(1, size)]
 
 
 def remote(src, dst, send_sem, recv_sem, axis, target):
@@ -56,6 +63,8 @@
     mp, dp = lax.axis_index("mp"), lax.axis_index("dp")
 
     half = nb // 2
+    others = partners(mp, M)
+    early = sum(1 for group in GROUPS if group[0] == 0)
     loads = []
     for src, dst, parts in (
         (a_hbm, a_v, 2), (r_hbm, r_v, 2), (l_hbm, l_v, 1), (g_hbm, g_v, 1)
@@ -85,8 +94,7 @@
     mine = pl.multiple_of(mp * nb, nb)
     forward = [[] for _ in range(NC)]
     def send_forward(c, start, size):
-        for s in range(1, M):
-            target = lax.rem(mp + s, M)
+        for s, target in enumerate(others, 1):
             base = target * nb + c * jc
 
             def pack(j, carry, base=base):
@@ -138,8 +146,8 @@
 
     back, sums_l = [[] for _ in range(len(GROUPS))], []
 
-    def turn(h, start, size, s):
-        base = lax.rem(mp + s, M) * nb + start
+    def turn(h, start, size, target):
+        base = target * nb + start
 
         def one(i, carry):
             part = gf32[pl.ds(h * hj * B + base + i, hj, stride=B), :]
@@ -160,9 +168,8 @@
 
     def turn_and_send(n):
         h, start, size = GROUPS[n]
-        for s in range(1, M):
-            turn(h, start, size, s)
-            target = lax.rem(mp + s, M)
+        for s, target in enumerate(others, 1):
+            turn(h, start, size, target)
             at_j = pl.multiple_of(mine + h * hj, hj)
             copy = remote(
                 gs.at[pl.ds(target * nb + start, size), pl.ds(h * hj, hj)],
@@ -196,12 +203,15 @@
             send_forward(c + AHEAD, 0, nb)
         else:
             turn_and_send(c + AHEAD - NC)
+            if c == NC - 1:
+                for n in range(AHEAD, early):
+                    turn_and_send(n)
         lax.fori_loop(c * jc, (c + 1) * jc, second, 0, unroll=2)
-        if c == 1:
+        if c == NC // H - 1:
             send_l(0)
             turn_own(0)
-    for n in range(AHEAD):
-        turn_and_send(AHEAD + n)
+    for n in range(BACK):
+        turn_and_send(early + n)
     send_l(1)
     turn_own(1)
 
@@ -223,7 +233,7 @@
     sums_r = []
 
     def send_r(g):
-        at = pl.ds(*GROUPS[AHEAD + g][1:])
+        at = pl.ds(*GROUPS[early + g][1:])
         step = []
         for s in range(1, D):
             target = lax.rem(dp + s, D)
@@ -247,22 +257,22 @@
         return carry
 
     def finish(g):
-        start, size = GROUPS[AHEAD + g][1:]
+        start, size = GROUPS[early + g][1:]
         for copy in sums_r[g]:
             copy.wait_recv()
         lax.fori_loop(start, start + size, add_r, 0, unroll=4)
 
-    count = len(GROUPS) - AHEAD
+    count = len(GROUPS) - early
     for g in range(count):
-        start, size = GROUPS[AHEAD + g][1:]
-        for n in range(AHEAD):
+        start, size = GROUPS[early + g][1:]
+        for n in range(early):
             if GROUPS[n][1] == start:
                 for copy in back[n]:
                     copy.wait_recv()
-        for copy in back[AHEAD + g]:
+        for copy in back[early + g]:
             copy.wait_recv()
-        if g + AHEAD < count:
-            turn_and_send(g + 2 * AHEAD)
+        if g + BACK < count:
+            turn_and_send(early + g + BACK)
         lax.fori_loop(start, start + size, last, 0, unroll=2)
         send_r(g)
         if g == 1:
@@ -293,13 +303,13 @@
     T = inputs.shape[1]
     rows = B // D
     scale = float(D * T) ** (-0.5)
-    NC, H = 4, 2
+    NC, H = 8, 2
     half, part, small = nb // 2, nb // 4, nb // 8
-    groups = ((0, 0, half), (0, half, half))
+    groups = tuple((0, n * part, part) for n in range(4))
     groups += ((1, 0, part), (1, part, part), (1, half, part))
     groups += ((1, half + part, small), (1, half + part + small, small))
     cfg = (M, D, nb, B, T, rows, scale, NC, H, groups)
-    count = len(groups) - AHEAD
+    count = sum(1 for group in groups if group[0] == 1)
     sem = pltpu.SemaphoreType.DMA
     flops = 6 * 2 * nb * B * B * T
     results = pl.pallas_call(
@@ -353,9 +363,10 @@
     outputs, grad_inputs, grad_r, grad_l = pl.pallas_call(
         write_out,
         out_shape=[jax.ShapeDtypeStruct(x.shape, x.dtype) for x in results],
-        in_specs=[pl.BlockSpec(memory_space=pltpu.VMEM)] * 4,
+        in_specs=[pl.BlockSpec(memory_space=pl.ANY)] * 4,
         out_specs=[pl.BlockSpec(memory_space=pltpu.HBM)] * 4,
         scratch_shapes=[sem((4,))],
+        compiler_params=pltpu.CompilerParams(vmem_limit_bytes=4 * 2**20),
         name="write_out",
     )(*results)
     return (

time: 68 us -> 63.7 us (0.937)
  local copies, waits for them, and re-layouts: 3.39 us -> 0 us
  Pallas kernels: 63.8 us -> 62.9 us
    unnamed x8 -> x0, local copies, waits for them, and re-layouts: 3.39 us -> none
    pallas_call x1, Pallas kernels: 3.17 us -> 1.52 us  [fused(): pl.pallas_call(write_out, out_shape=[jax.ShapeDtypeStruct(x.shape, x.dtyp...]
    pallas_call x1, Pallas kernels: 60.6 us -> 61.4 us  [fused(): pl.pallas_call(functools.partial(kernel, cfg), out_shape=(pltpu.VMEM((nb,...]
where the time goes in v6:
time: 63.7 us; the launch traced here: 63.5 us
  Pallas kernels  62.9 us (99%)
  between operations  0.64 us (1%)
    pallas_call x1, Pallas kernels, fused(): pl.pallas_call(functools.partial(kernel, cfg), out_shape=(pltpu.VMEM((nb,...  61.4 us
    pallas_call x1, Pallas kernels, fused(): pl.pallas_call(write_out, out_shape=[jax.ShapeDtypeStruct(x.shape, x.dtyp...  1.52 us

profile of v6, /device:TPU:0, one launch (start us, length us, event | category | flops | bytes accessed | tf_op | source)
XLA Modules:
  0.0 63.5 jit_solution(6770114752826446648)
XLA Ops:
  0.6 61.4 %monarch.1 = (bf16[32,128,128]{2,1,0:T(8,128)(2,1)S(1)}, bf16[32,128,128]{2,1,0:T(8,128)(2,1)S(1)}, f32[32,16,128]{2,1,0:T(8,128)S(1)}, f32[32,16,128]{2,1,0:T(8,128)S(1)}) custom-call(bf16[32,128,128]{2,1,0:T(8,128)(2,1)} %bitcast.8, bf16[32,128,128]{2,1,0:T(8,128)(2,1)} %bitcast.9, bf16[32,128,128]{2,1,0:T(8,128)(2,1)} %bitcast.10, ...), custom_call_target="tpu_custom_call" | custom-call | flops 805306368 | bytes 8388608 | tf_op jit(solution)/shard_map/monarch/pallas_call | solution.py:315
  62.0 1.5 %write_out.1 = (bf16[32,128,128]{2,1,0:T(8,128)(2,1)}, bf16[32,128,128]{2,1,0:T(8,128)(2,1)}, f32[32,16,128]{2,1,0:T(8,128)}, f32[32,16,128]{2,1,0:T(8,128)}) custom-call(bf16[32,128,128]{2,1,0:T(8,128)(2,1)S(1)} %get-tuple-element.12.refs_0_, bf16[32,128,128]{2,1,0:T(8,128)(2,1)S(1)} %get-tuple-element.13.refs_1_, ...), custom_call_target="tpu_custom_call" | custom-call | tf_op jit(solution)/shard_map/write_out/pallas_call | solution.py:363

commit v7 on v6

--- a/solution.py
+++ b/solution.py
@@ -10,7 +10,7 @@
 MESH = pl.DeviceIdType.MESH
 F32 = jnp.float32
 BF16 = jnp.bfloat16
-AHEAD = 3
+AHEAD = 2
 BACK = 2
 
 
@@ -102,7 +102,7 @@
                 fs[base + j, pl.ds(start, size), :] = fo32[pl.ds(at, size), :].astype(BF16)
                 return carry
 
-            lax.fori_loop(0, jc, pack, 0, unroll=4)
+            lax.fori_loop(0, jc, pack, 0, unroll=8)
             slot = c * 2 + start // half
             copy = remote(
                 fs.at[pl.ds(base, jc), pl.ds(start, size)],
@@ -118,7 +118,7 @@
     for p in range(2):
         loads[p].wait()
         loads[2 + p].wait()
-        lax.fori_loop(p * half, (p + 1) * half, first, 0, unroll=4)
+        lax.fori_loop(p * half, (p + 1) * half, first, 0, unroll=8)
         if p == 0:
             pl.semaphore_wait(barrier, (M - 1) + (D - 1))
         for c in range(AHEAD):
@@ -154,7 +154,7 @@
             gs[base + i, pl.ds(h * hj, hj), :] = part.astype(BF16)
             return carry
 
-        lax.fori_loop(0, size, one, 0, unroll=4)
+        lax.fori_loop(0, size, one, 0, unroll=8)
 
     def turn_own(h):
         at_j = pl.multiple_of(mine + h * hj, hj)
@@ -164,7 +164,7 @@
             gb[i, pl.ds(at_j, hj), :] = part.astype(BF16)
             return carry
 
-        lax.fori_loop(0, nb, one, 0, unroll=4)
+        lax.fori_loop(0, nb, one, 0, unroll=8)
 
     def turn_and_send(n):
         h, start, size = GROUPS[n]
@@ -206,7 +206,7 @@
             if c == NC - 1:
                 for n in range(AHEAD, early):
                     turn_and_send(n)
-        lax.fori_loop(c * jc, (c + 1) * jc, second, 0, unroll=2)
+        lax.fori_loop(c * jc, (c + 1) * jc, second, 0, unroll=4)
         if c == NC // H - 1:
             send_l(0)
             turn_own(0)
@@ -273,7 +273,7 @@
             copy.wait_recv()
         if g + BACK < count:
             turn_and_send(early + g + BACK)
-        lax.fori_loop(start, start + size, last, 0, unroll=2)
+        lax.fori_loop(start, start + size, last, 0, unroll=4)
         send_r(g)
         if g == 1:
             for copy in sums_l:
@@ -303,9 +303,9 @@
     T = inputs.shape[1]
     rows = B // D
     scale = float(D * T) ** (-0.5)
-    NC, H = 8, 2
+    NC, H = 4, 2
     half, part, small = nb // 2, nb // 4, nb // 8
-    groups = tuple((0, n * part, part) for n in range(4))
+    groups = ((0, 0, half), (0, half, half))
     groups += ((1, 0, part), (1, part, part), (1, half, part))
     groups += ((1, half + part, small), (1, half + part + small, small))
     cfg = (M, D, nb, B, T, rows, scale, NC, H, groups)

time: 63.7 us -> 64 us (level)
  no operation moved by 1% of the time
where the time goes in v7:
time: 64 us; the launch traced here: 63.8 us
  Pallas kernels  63.2 us (99%)
  between operations  0.64 us (1%)
    pallas_call x1, Pallas kernels, fused(): pl.pallas_call(functools.partial(kernel, cfg), out_shape=(pltpu.VMEM((nb,...  61.7 us
    pallas_call x1, Pallas kernels, fused(): pl.pallas_call(write_out, out_shape=[jax.ShapeDtypeStruct(x.shape, x.dtyp...  1.52 us

profile of v7, /device:TPU:0, one launch (start us, length us, event | category | flops | bytes accessed | tf_op | source)
XLA Modules:
  0.0 63.8 jit_solution(11296716476116014604)
XLA Ops:
  0.6 61.7 %monarch.1 = (bf16[32,128,128]{2,1,0:T(8,128)(2,1)S(1)}, bf16[32,128,128]{2,1,0:T(8,128)(2,1)S(1)}, f32[32,16,128]{2,1,0:T(8,128)S(1)}, f32[32,16,128]{2,1,0:T(8,128)S(1)}) custom-call(bf16[32,128,128]{2,1,0:T(8,128)(2,1)} %bitcast.8, bf16[32,128,128]{2,1,0:T(8,128)(2,1)} %bitcast.9, bf16[32,128,128]{2,1,0:T(8,128)(2,1)} %bitcast.10, ...), custom_call_target="tpu_custom_call" | custom-call | flops 805306368 | bytes 8388608 | tf_op jit(solution)/shard_map/monarch/pallas_call | solution.py:315
  62.3 1.5 %write_out.1 = (bf16[32,128,128]{2,1,0:T(8,128)(2,1)}, bf16[32,128,128]{2,1,0:T(8,128)(2,1)}, f32[32,16,128]{2,1,0:T(8,128)}, f32[32,16,128]{2,1,0:T(8,128)}) custom-call(bf16[32,128,128]{2,1,0:T(8,128)(2,1)S(1)} %get-tuple-element.12.refs_0_, bf16[32,128,128]{2,1,0:T(8,128)(2,1)S(1)} %get-tuple-element.13.refs_1_, ...), custom_call_target="tpu_custom_call" | custom-call | tf_op jit(solution)/shard_map/write_out/pallas_call | solution.py:363

commit v8 on v7

--- a/solution.py
+++ b/solution.py
@@ -27,12 +27,6 @@
     half = 0.5 + 0.5 * tanh
     slope = half + 0.5 * v * (1.0 - tanh * tanh) * (c0 + (3.0 * c0 * c1) * square)
     return v * half, slope
-
-
-def partners(me, size):
-    if size == 4:
-        return [lax.rem(me + 2, 4), 3 - me, me + 1 - 2 * lax.rem(me, 2)]
-    return [lax.rem(me + s, size) for s in range(1, size)]
 
 
 def remote(src, dst, send_sem, recv_sem, axis, target):
@@ -63,7 +57,7 @@
     mp, dp = lax.axis_index("mp"), lax.axis_index("dp")
 
     half = nb // 2
-    others = partners(mp, M)
+    others = [lax.rem(mp + s, M) for s in range(1, M)]
     early = sum(1 for group in GROUPS if group[0] == 0)
     loads = []
     for src, dst, parts in (
@@ -91,24 +85,27 @@
         fo32[pl.ds(i, B, stride=nb), :] = dot(r_v[i], a_v[i], 0, 0)
         return carry
 
-    mine = pl.multiple_of(mp * nb, nb)
+    mine = mp * nb
     forward = [[] for _ in range(NC)]
-    def send_forward(c, start, size):
+    def pack_one(dst, j, row, p):
+        at = pl.multiple_of(j * nb + p * half, half)
+        dst[p, row] = fo32[pl.ds(at, half), :].astype(BF16)
+
+    def send_forward(c, first_part, parts):
         for s, target in enumerate(others, 1):
             base = target * nb + c * jc
 
             def pack(j, carry, base=base):
-                at = pl.multiple_of((base + j) * nb + start, half)
-                fs[base + j, pl.ds(start, size), :] = fo32[pl.ds(at, size), :].astype(BF16)
+                for p in range(first_part, first_part + parts):
+                    pack_one(fs, base + j, base + j, p)
                 return carry
 
-            lax.fori_loop(0, jc, pack, 0, unroll=8)
-            slot = c * 2 + start // half
+            lax.fori_loop(0, jc, pack, 0, unroll=4)
             copy = remote(
-                fs.at[pl.ds(base, jc), pl.ds(start, size)],
-                fr.at[pl.ds(c * jc, jc), pl.ds(pl.multiple_of(mine + start, half), size)],
-                fs_sem.at[slot, s - 1],
-                fr_sem.at[slot, s - 1],
+                fs.at[pl.ds(first_part, parts), pl.ds(base, jc)],
+                fr.at[mp, pl.ds(first_part, parts), pl.ds(c * jc, jc)],
+                fs_sem.at[c * 2 + first_part, s - 1],
+                fr_sem.at[c * 2 + first_part, s - 1],
                 "mp",
                 target,
             )
@@ -122,11 +119,11 @@
         if p == 0:
             pl.semaphore_wait(barrier, (M - 1) + (D - 1))
         for c in range(AHEAD):
-            send_forward(c, p * half, half)
+            send_forward(c, p, 1)
 
     def own(j, carry):
-        at = pl.multiple_of((mine + j) * nb, nb)
-        fr[j, pl.ds(mine, nb), :] = fo32[pl.ds(at, nb), :].astype(BF16)
+        for p in range(2):
+            pack_one(fr.at[mp], mine + j, j, p)
         return carry
 
     lax.fori_loop(0, nb, own, 0, unroll=4)
@@ -134,7 +131,7 @@
     loads[5].wait()
 
     def second(jj, carry):
-        x, left = fr[jj], l_v[jj]
+        x, left = fr[:, :, jj].reshape(B, T), l_v[jj]
         value, slope = gelu_and_slope(dot(left, x, 0, 0))
         out_v[jj] = value.astype(BF16)
         grad_pre = (g_v[jj].astype(F32) * slope).astype(BF16)
@@ -151,17 +148,15 @@
 
         def one(i, carry):
             part = gf32[pl.ds(h * hj * B + base + i, hj, stride=B), :]
-            gs[base + i, pl.ds(h * hj, hj), :] = part.astype(BF16)
+            gs[h, base + i] = part.astype(BF16)
             return carry
 
         lax.fori_loop(0, size, one, 0, unroll=8)
 
     def turn_own(h):
-        at_j = pl.multiple_of(mine + h * hj, hj)
-
         def one(i, carry):
             part = gf32[pl.ds(h * hj * B + mine + i, hj, stride=B), :]
-            gb[i, pl.ds(at_j, hj), :] = part.astype(BF16)
+            gb[mp, h, i] = part.astype(BF16)
             return carry
 
         lax.fori_loop(0, nb, one, 0, unroll=8)
@@ -170,10 +165,9 @@
         h, start, size = GROUPS[n]
         for s, target in enumerate(others, 1):
             turn(h, start, size, target)
-            at_j = pl.multiple_of(mine + h * hj, hj)
             copy = remote(
-                gs.at[pl.ds(target * nb + start, size), pl.ds(h * hj, hj)],
-                gb.at[pl.ds(start, size), pl.ds(at_j, hj)],
+                gs.at[h, pl.ds(target * nb + start, size)],
+                gb.at[mp, h, pl.ds(start, size)],
                 gs_sem.at[n, s - 1],
                 gb_sem.at[n, s - 1],
                 "mp",
@@ -200,7 +194,7 @@
         for copy in forward[c]:
             copy.wait_recv()
         if c + AHEAD < NC:
-            send_forward(c + AHEAD, 0, nb)
+            send_forward(c + AHEAD, 0, 2)
         else:
             turn_and_send(c + AHEAD - NC)
             if c == NC - 1:
@@ -223,7 +217,7 @@
         return carry
 
     def last(ii, carry):
-        y = gb[ii]
+        y = gb[:, :, ii].reshape(B, T)
         gi_v[ii] = dot(r_v[ii], y, 1, 0).astype(BF16)
         term = (dot(a_v[ii], y, 1, 1) * scale).astype(BF16)
         for d in range(D):
@@ -328,11 +322,11 @@
             pltpu.VMEM((nb, B, B), BF16),
             pltpu.VMEM((nb, B, B), BF16),
             pltpu.VMEM((B * nb, T), F32),
-            pltpu.VMEM((B, nb, T), BF16),
-            pltpu.VMEM((nb, B, T), BF16),
+            pltpu.VMEM((2, B, half, T), BF16),
+            pltpu.VMEM((M, 2, nb, half, T), BF16),
             pltpu.VMEM((nb * B, T), F32),
-            pltpu.VMEM((B, nb, T), BF16),
-            pltpu.VMEM((nb, B, T), BF16),
+            pltpu.VMEM((H, B, nb // H, T), BF16),
+            pltpu.VMEM((M, H, nb, nb // H, T), BF16),
             pltpu.VMEM((D, nb, rows, B), BF16),
             pltpu.VMEM((D - 1, nb, rows, B), BF16),
             pltpu.VMEM((D, nb, rows, B), BF16),

time: 64 us -> 63.1 us (0.986)
  Pallas kernels: 63.2 us -> 62.3 us
    pallas_call x1, Pallas kernels: 61.7 us -> 60.8 us  [fused(): pl.pallas_call(functools.partial(kernel, cfg), out_shape=(pltpu.VMEM((nb,...]
where the time goes in v8:
time: 63.1 us; the launch traced here: 63 us
  Pallas kernels  62.3 us (99%)
  between operations  0.64 us (1%)
    pallas_call x1, Pallas kernels, fused(): pl.pallas_call(functools.partial(kernel, cfg), out_shape=(pltpu.VMEM((nb,...  60.8 us
    pallas_call x1, Pallas kernels, fused(): pl.pallas_call(write_out, out_shape=[jax.ShapeDtypeStruct(x.shape, x.dtyp...  1.52 us

profile of v8, /device:TPU:0, one launch (start us, length us, event | category | flops | bytes accessed | tf_op | source)
XLA Modules:
  0.0 63.0 jit_solution(384206977539037250)
XLA Ops:
  0.6 60.8 %monarch.1 = (bf16[32,128,128]{2,1,0:T(8,128)(2,1)S(1)}, bf16[32,128,128]{2,1,0:T(8,128)(2,1)S(1)}, f32[32,16,128]{2,1,0:T(8,128)S(1)}, f32[32,16,128]{2,1,0:T(8,128)S(1)}) custom-call(bf16[32,128,128]{2,1,0:T(8,128)(2,1)} %bitcast.8, bf16[32,128,128]{2,1,0:T(8,128)(2,1)} %bitcast.9, bf16[32,128,128]{2,1,0:T(8,128)(2,1)} %bitcast.10, ...), custom_call_target="tpu_custom_call" | custom-call | flops 805306368 | bytes 8388608 | tf_op jit(solution)/shard_map/monarch/pallas_call | solution.py:309
  61.4 1.5 %write_out.1 = (bf16[32,128,128]{2,1,0:T(8,128)(2,1)}, bf16[32,128,128]{2,1,0:T(8,128)(2,1)}, f32[32,16,128]{2,1,0:T(8,128)}, f32[32,16,128]{2,1,0:T(8,128)}) custom-call(bf16[32,128,128]{2,1,0:T(8,128)(2,1)S(1)} %get-tuple-element.12.refs_0_, bf16[32,128,128]{2,1,0:T(8,128)(2,1)S(1)} %get-tuple-element.13.refs_1_, ...), custom_call_target="tpu_custom_call" | custom-call | tf_op jit(solution)/shard_map/write_out/pallas_call | solution.py:357

commit v9 on v8

--- a/solution.py
+++ b/solution.py
@@ -57,7 +57,8 @@
     mp, dp = lax.axis_index("mp"), lax.axis_index("dp")
 
     half = nb // 2
-    others = [lax.rem(mp + s, M) for s in range(1, M)]
+    turns = [1 + lax.rem(n + lax.rem(dp, 2), M - 1) for n in range(M - 1)]
+    others = [(s, lax.rem(mp + s, M)) for s in turns]
     early = sum(1 for group in GROUPS if group[0] == 0)
     loads = []
     for src, dst, parts in (
@@ -92,7 +93,7 @@
         dst[p, row] = fo32[pl.ds(at, half), :].astype(BF16)
 
     def send_forward(c, first_part, parts):
-        for s, target in enumerate(others, 1):
+        for s, target in others:
             base = target * nb + c * jc
 
             def pack(j, carry, base=base):
@@ -163,7 +164,7 @@
 
     def turn_and_send(n):
         h, start, size = GROUPS[n]
-        for s, target in enumerate(others, 1):
+        for s, target in others:
             turn(h, start, size, target)
             copy = remote(
                 gs.at[h, pl.ds(target * nb + start, size)],
@@ -406,7 +407,7 @@
 
     def shards(inputs, cotangent, r_factor, l_factor):
         nb, B = r_factor.shape[1], r_factor.shape[2]
-        tiled = nb % 32 == 0 and (B // D) % 16 == 0 and M > 1 and D > 1
+        tiled = nb % 32 == 0 and (B // D) % 16 == 0 and M > 2 and D > 1
         return (fused if tiled else plain)(M, D, inputs, cotangent, r_factor, l_factor)
 
     return jax.shard_map(

time: 63.1 us -> 64 us (1.014)
  Pallas kernels: 62.3 us -> 63.2 us
    pallas_call x1, Pallas kernels: 60.8 us -> 61.7 us  [fused(): pl.pallas_call(functools.partial(kernel, cfg), out_shape=(pltpu.VMEM((nb,...]
where the time goes in v9:
time: 64 us; the launch traced here: 63.8 us
  Pallas kernels  63.2 us (99%)
  between operations  0.64 us (1%)
    pallas_call x1, Pallas kernels, fused(): pl.pallas_call(functools.partial(kernel, cfg), out_shape=(pltpu.VMEM((nb,...  61.7 us
    pallas_call x1, Pallas kernels, fused(): pl.pallas_call(write_out, out_shape=[jax.ShapeDtypeStruct(x.shape, x.dtyp...  1.52 us

profile of v9, /device:TPU:0, one launch (start us, length us, event | category | flops | bytes accessed | tf_op | source)
XLA Modules:
  0.0 63.8 jit_solution(1610739235223426713)
XLA Ops:
  0.6 61.7 %monarch.1 = (bf16[32,128,128]{2,1,0:T(8,128)(2,1)S(1)}, bf16[32,128,128]{2,1,0:T(8,128)(2,1)S(1)}, f32[32,16,128]{2,1,0:T(8,128)S(1)}, f32[32,16,128]{2,1,0:T(8,128)S(1)}) custom-call(bf16[32,128,128]{2,1,0:T(8,128)(2,1)} %bitcast.8, bf16[32,128,128]{2,1,0:T(8,128)(2,1)} %bitcast.9, bf16[32,128,128]{2,1,0:T(8,128)(2,1)} %bitcast.10, ...), custom_call_target="tpu_custom_call" | custom-call | flops 805306368 | bytes 8388608 | tf_op jit(solution)/shard_map/monarch/pallas_call | solution.py:310
  62.3 1.5 %write_out.1 = (bf16[32,128,128]{2,1,0:T(8,128)(2,1)}, bf16[32,128,128]{2,1,0:T(8,128)(2,1)}, f32[32,16,128]{2,1,0:T(8,128)}, f32[32,16,128]{2,1,0:T(8,128)}) custom-call(bf16[32,128,128]{2,1,0:T(8,128)(2,1)S(1)} %get-tuple-element.12.refs_0_, bf16[32,128,128]{2,1,0:T(8,128)(2,1)S(1)} %get-tuple-element.13.refs_1_, ...), custom_call_target="tpu_custom_call" | custom-call | tf_op jit(solution)/shard_map/write_out/pallas_call | solution.py:358
